TPU v7x, 32 devices: a whole 2x2x4 slice. The times are simulated.
32 devices in a mesh: fsdp: 4 (over z), ctx: 4 (over y, x), tp: 2 (over core).
Axes of the slice: x: 2, y: 2, z: 4, core: 2. Of those that a mesh axis runs over, the one named last changes fastest.
Arguments:
- layer_input: bfloat16 [8, 512, 768], P('fsdp', 'ctx'), may hold values from -6 to 6
- lengths: int32 [8], P('fsdp'), may hold values from 1 to 512, as said below
- first_gain: float32 [768], replicated, may hold values from 0.1 to 1.9
- first_shift: float32 [768], replicated, may hold values from -3 to 3
- qkv_weight: bfloat16 [3, 768, 768], P(None, ('fsdp', 'ctx'), 'tp'), may hold values from -0.3125 to 0.3125
- qv_bias: float32 [2, 768], P(None, 'tp'), may hold values from -3 to 3
- out_weight: bfloat16 [768, 768], P('tp', ('fsdp', 'ctx')), may hold values from -0.875 to 0.875
- out_bias: float32 [768], replicated, may hold values from -3 to 3
- second_gain: float32 [768], replicated, may hold values from 0.1 to 1.9
- second_shift: float32 [768], replicated, may hold values from -3 to 3
- up_weight: bfloat16 [768, 3072], P(('fsdp', 'ctx'), 'tp'), may hold values from -0.21875 to 0.21875
- up_bias: float32 [3072], P('tp'), may hold values from -3 to 3
- down_weight: bfloat16 [3072, 768], P('tp', ('fsdp', 'ctx')), may hold values from -0.109375 to 0.109375
- down_bias: float32 [768], replicated, may hold values from -3 to 3
- cotangent: bfloat16 [8, 512, 768], P('fsdp', 'ctx'), may hold values from -8 to 8
Outputs:
- layer_output: bfloat16 [8, 512, 768], P('fsdp', 'ctx')
- grad_input: float32 [8, 512, 768], P('fsdp', 'ctx')
- grad_firstgain: float32 [768], replicated
- grad_firstshift: float32 [768], replicated
- grad_qkvweight: float32 [3, 768, 768], P(None, ('fsdp', 'ctx'), 'tp')
- grad_qvbias: float32 [2, 768], P(None, 'tp')
- grad_outweight: float32 [768, 768], P('tp', ('fsdp', 'ctx'))
- grad_outbias: float32 [768], replicated
- grad_secondgain: float32 [768], replicated
- grad_secondshift: float32 [768], replicated
- grad_upweight: float32 [768, 3072], P(('fsdp', 'ctx'), 'tp')
- grad_upbias: float32 [3072], P('tp')
- grad_downweight: float32 [3072, 768], P('tp', ('fsdp', 'ctx'))
- grad_downbias: float32 [768], replicated
Inputs may be any that keep to these rules, and one draw needn't show every extreme that they name: `lengths`: in the 2 sequences of each index of fsdp, one, chosen at random, has exactly 512 valid positions.
All inputs are finite; a program needn't handle non-finite values.
Results may differ from a plain program's by a relative error of at most 0.01.
The roundings to bfloat16 on the way count: a program that leaves them out, or rounds other values in their place, can miss the bound.
Values may be sent and summed in bfloat16 or wider, within the bound.
A program may use at most 128 MiB of HBM per device.

v0:
```python
import math

import jax
import jax.numpy as jnp
from jax import lax
from jax.sharding import PartitionSpec as P

HEAD = 64


def norm_rows(rows_in, row_gain, row_shift):
    centre_mean = jnp.mean(rows_in, axis=-1, keepdims=True)
    centred = rows_in - centre_mean
    variance = jnp.mean(centred * centred, axis=-1, keepdims=True)
    return centred * lax.rsqrt(variance + 1e-05) * row_gain + row_shift


def head_sum(pieces):
    shares = lax.psum_scatter(pieces, "tp", scatter_dimension=0, tiled=True)
    return lax.all_gather(shares, "tp", axis=0, tiled=True)


def body(
    layer_input,
    lengths,
    first_gain,
    first_shift,
    qkv_weight,
    qv_bias,
    out_weight,
    out_bias,
    second_gain,
    second_shift,
    up_weight,
    up_bias,
    down_weight,
    down_bias,
    cotangent,
):
    seq_count, span, width = layer_input.shape
    row_count = seq_count * span
    local_width = qkv_weight.shape[2]
    head_count = local_width // HEAD
    full_length = span * lax.axis_size("ctx")
    score_scale = 1.0 / math.sqrt(HEAD)
    f32 = jnp.float32
    bf16 = jnp.bfloat16
    inputs = layer_input.astype(f32).reshape(row_count, width)
    qkv_full, out_full, up_full, down_full = (
        lax.all_gather(qkv_weight, ("fsdp", "ctx"), axis=1, tiled=True),
        lax.all_gather(out_weight, ("fsdp", "ctx"), axis=1, tiled=True),
        lax.all_gather(up_weight, ("fsdp", "ctx"), axis=0, tiled=True),
        lax.all_gather(down_weight, ("fsdp", "ctx"), axis=1, tiled=True),
    )
    normed_low = norm_rows(inputs, first_gain, first_shift).astype(bf16)
    projected = jnp.einsum("rd,kdc->krc", normed_low, qkv_full, preferred_element_type=f32)
    queries = (projected[0] + qv_bias[0]).astype(bf16)
    key_local = projected[1].astype(bf16).reshape(seq_count, span, local_width)
    value_local = (projected[2] + qv_bias[1]).astype(bf16).reshape(seq_count, span, local_width)
    key_all, value_all = (
        lax.all_gather(key_local, "ctx", axis=1, tiled=True),
        lax.all_gather(value_local, "ctx", axis=1, tiled=True),
    )
    query_heads = queries.reshape(seq_count, span, head_count, HEAD)
    query_pos = lax.axis_index("ctx") * span + jnp.arange(span, dtype=jnp.int32)
    key_pos = jnp.arange(full_length, dtype=jnp.int32)
    allowed = (key_pos[None, :] <= query_pos[:, None])[None, None] & (
        key_pos[None, None, None, :] < lengths[:, None, None, None]
    )

    def masked_scores(key_source):
        key_heads = key_source.reshape(seq_count, full_length, head_count, HEAD)
        scores = (
            jnp.einsum("suhe,snhe->shun", query_heads, key_heads, preferred_element_type=f32)
            * score_scale
        )
        return jnp.where(allowed, scores, -1e30)

    masked = masked_scores(key_all)
    peak = jnp.max(masked, axis=-1, keepdims=True)
    expo = jnp.where(allowed, jnp.exp(masked - peak), 0.0)
    row_total = jnp.sum(expo, axis=-1, keepdims=True)
    log_total = peak + jnp.log(row_total)
    probs_low = (expo / row_total).astype(bf16)
    value_heads = value_all.reshape(seq_count, full_length, head_count, HEAD)
    attended = jnp.einsum("shun,snhe->suhe", probs_low, value_heads, preferred_element_type=f32)
    attended = attended.reshape(row_count, local_width).astype(bf16)
    residual = inputs + head_sum(jnp.dot(attended, out_full, preferred_element_type=f32)) + out_bias
    normed_two_low = norm_rows(residual, second_gain, second_shift).astype(bf16)
    up_proj = jnp.dot(normed_two_low, up_full, preferred_element_type=f32) + up_bias
    activated_low = jax.nn.gelu(up_proj, approximate=True).astype(bf16)
    mixed = head_sum(jnp.dot(activated_low, down_full, preferred_element_type=f32))
    layer_output = (residual + mixed + down_bias).astype(bf16).reshape(seq_count, span, width)
    qkv_back, out_back, up_back, down_back = (
        lax.all_gather(qkv_weight, ("fsdp", "ctx"), axis=1, tiled=True),
        lax.all_gather(out_weight, ("fsdp", "ctx"), axis=1, tiled=True),
        lax.all_gather(up_weight, ("fsdp", "ctx"), axis=0, tiled=True),
        lax.all_gather(down_weight, ("fsdp", "ctx"), axis=1, tiled=True),
    )
    key_back, value_back = (
        lax.all_gather(key_local, "ctx", axis=1, tiled=True),
        lax.all_gather(value_local, "ctx", axis=1, tiled=True),
    )
    grad_out = cotangent.reshape(row_count, width)
    grad_downbias = jnp.sum(grad_out.astype(f32), axis=0)
    grad_downweight = jnp.einsum("rf,rd->fd", activated_low, grad_out, preferred_element_type=f32)
    grad_act = jnp.einsum("rd,fd->rf", grad_out, down_back, preferred_element_type=f32)
    gelu_back = jax.vjp(lambda z: jax.nn.gelu(z, approximate=True), up_proj)[1]
    grad_up = gelu_back(grad_act)[0].astype(bf16)
    grad_upbias = jnp.sum(grad_up.astype(f32), axis=0)
    grad_upweight = jnp.einsum("rd,rf->df", normed_two_low, grad_up, preferred_element_type=f32)
    grad_normtwo = head_sum(jnp.einsum("rf,df->rd", grad_up, up_back, preferred_element_type=f32))
    second_back = jax.vjp(norm_rows, residual, second_gain, second_shift)[1]
    grad_resid_norm, grad_secondgain, grad_secondshift = second_back(grad_normtwo)
    grad_residual = grad_out.astype(f32) + grad_resid_norm
    grad_branch = grad_residual.astype(bf16)
    grad_outbias = jnp.sum(grad_branch.astype(f32), axis=0)
    grad_outweight = jnp.einsum("rc,rd->cd", attended, grad_branch, preferred_element_type=f32)
    grad_attended = jnp.einsum(
        "rd,cd->rc", grad_branch, out_back, preferred_element_type=f32
    ).astype(bf16)
    masked_again = masked_scores(key_back)
    probs_again = jnp.where(allowed, jnp.exp(masked_again - log_total), 0.0)
    probs_low_again = probs_again.astype(bf16)
    key_heads_back = key_back.reshape(seq_count, full_length, head_count, HEAD)
    value_heads_back = value_back.reshape(seq_count, full_length, head_count, HEAD)
    grad_att_heads = grad_attended.reshape(seq_count, span, head_count, HEAD)
    grad_probs = jnp.einsum(
        "suhe,snhe->shun", grad_att_heads, value_heads_back, preferred_element_type=f32
    )
    inner_total = jnp.sum(probs_again * grad_probs, axis=-1, keepdims=True)
    grad_scores = (probs_again * (grad_probs - inner_total)).astype(bf16)
    grad_query = (
        jnp.einsum("shun,snhe->suhe", grad_scores, key_heads_back, preferred_element_type=f32)
        * score_scale
    )
    grad_query = grad_query.astype(bf16).reshape(row_count, local_width)
    amount = lax.axis_size("ctx") * span
    key_part = (
        jnp.einsum("shun,suhe->nshe", grad_scores, query_heads, preferred_element_type=f32)
        * score_scale
    )
    value_part = jnp.einsum(
        "shun,suhe->nshe", probs_low_again, grad_att_heads, preferred_element_type=f32
    )
    key_grads = lax.psum_scatter(
        jnp.concatenate(
            (
                key_part.reshape(amount, seq_count, local_width),
                value_part.reshape(amount, seq_count, local_width),
            ),
            axis=2,
        ),
        "ctx",
        scatter_dimension=0,
        tiled=True,
    )
    grad_key = (
        jnp.transpose(key_grads[:, :, :local_width], (1, 0, 2))
        .astype(bf16)
        .reshape(row_count, local_width)
    )
    grad_value = (
        jnp.transpose(key_grads[:, :, local_width:], (1, 0, 2))
        .astype(bf16)
        .reshape(row_count, local_width)
    )
    grad_proj = jnp.stack((grad_query, grad_key, grad_value))
    grad_qvbias = jnp.stack(
        (jnp.sum(grad_query.astype(f32), axis=0), jnp.sum(grad_value.astype(f32), axis=0))
    )
    grad_qkvweight = jnp.einsum("rd,krc->kdc", normed_low, grad_proj, preferred_element_type=f32)
    grad_normed = head_sum(
        jnp.einsum("krc,kdc->rd", grad_proj, qkv_back, preferred_element_type=f32)
    )
    first_back = jax.vjp(norm_rows, inputs, first_gain, first_shift)[1]
    grad_in_norm, grad_firstgain, grad_firstshift = first_back(grad_normed)
    grad_input = (grad_residual + grad_in_norm).reshape(seq_count, span, width)
    weight_grads = (
        lax.psum_scatter(grad_qkvweight, ("fsdp", "ctx"), scatter_dimension=1, tiled=True),
        lax.psum_scatter(grad_outweight, ("fsdp", "ctx"), scatter_dimension=1, tiled=True),
        lax.psum_scatter(grad_upweight, ("fsdp", "ctx"), scatter_dimension=0, tiled=True),
        lax.psum_scatter(grad_downweight, ("fsdp", "ctx"), scatter_dimension=1, tiled=True),
    )
    small_sums = lax.psum(
        (
            grad_firstgain,
            grad_firstshift,
            grad_qvbias,
            grad_outbias,
            grad_secondgain,
            grad_secondshift,
            grad_upbias,
            grad_downbias,
        ),
        ("fsdp", "ctx"),
    )
    return (
        layer_output,
        grad_input,
        small_sums[0],
        small_sums[1],
        weight_grads[0],
        small_sums[2],
        weight_grads[1],
        small_sums[3],
        small_sums[4],
        small_sums[5],
        weight_grads[2],
        small_sums[6],
        weight_grads[3],
        small_sums[7],
    )


def solution(mesh):
    in_specs = (
        P("fsdp", "ctx", None),
        P("fsdp"),
        P(),
        P(),
        P(None, ("fsdp", "ctx"), "tp"),
        P(None, "tp"),
        P("tp", ("fsdp", "ctx")),
        P(),
        P(),
        P(),
        P(("fsdp", "ctx"), "tp"),
        P("tp"),
        P("tp", ("fsdp", "ctx")),
        P(),
        P("fsdp", "ctx", None),
    )
    out_specs = (
        P("fsdp", "ctx", None),
        P("fsdp", "ctx", None),
        P(),
        P(),
        P(None, ("fsdp", "ctx"), "tp"),
        P(None, "tp"),
        P("tp", ("fsdp", "ctx")),
        P(),
        P(),
        P(),
        P(("fsdp", "ctx"), "tp"),
        P("tp"),
        P("tp", ("fsdp", "ctx")),
        P(),
    )
    return jax.shard_map(body, mesh=mesh, in_specs=in_specs, out_specs=out_specs, check_vma=False)
```

profile of v0, /device:TPU:0, one launch (start us, length us, event | category | flops | bytes accessed | tf_op | source)
XLA Modules:
  0.0 927.0 jit_solution(18336864054075329796)
XLA Ops:
  15.4 49.5 %all_gather.39 = bf16[384,768]{0,1:T(8,128)(2,1)} all-gather(bf16[384,48]{0,1:T(8,128)(2,1)S(1)} %copy-done.34), channel_id=1, replica_groups=mesh['fsdp'=4,'ctx'=4,'tp'=2] {'fsdp','ctx'}, dimensions={1}, use_global_device_ids=true | all-gather | bytes 626688 | tf_op jit(solution)/shard_map/all_gather | solution.py:51
  64.9 8.9 all-gather.4.cloned.1.call-done
  73.8 2.2 convolution_bitcast_fusion.1
  76.5 13.0 %all_gather.38 = bf16[2,512,384]{2,1,0:T(8,128)(2,1)S(1)} all-gather(bf16[2,128,384]{2,1,0:T(8,128)(2,1)S(1)} %bitcast.130), channel_id=1, replica_groups=mesh['fsdp'=4,'ctx'=4,'tp'=2] {'ctx'}, dimensions={1}, use_global_device_ids=true | all-gather | bytes 983040 | tf_op jit(solution)/shard_map/all_gather | solution.py:61
  90.7 9.6 %all_gather.37 = bf16[2,512,384]{2,1,0:T(8,128)(2,1)S(1)} all-gather(bf16[2,128,384]{2,1,0:T(8,128)(2,1)S(1)} %add_convert_fusion.2), channel_id=1, replica_groups=mesh['fsdp'=4,'ctx'=4,'tp'=2] {'ctx'}, dimensions={1}, use_global_device_ids=true | all-gather | bytes 983040 | tf_op jit(solution)/shard_map/all_gather | solution.py:62
  101.5 2.1 fusion.1
  108.8 29.2 %all-gather.8.cloned.1.call-done = bf16[1536,768]{0,1:T(8,128)(2,1)} async-done(((bf16[1536,48]{0,1:T(8,128)(2,1)}), bf16[1536,768]{0,1:T(8,128)(2,1)}) %all-gather.8.cloned.1.call-update) | async-done | bytes 2359312 | tf_op jit(solution)/shard_map/all_gather | solution.py:53
  138.0 3.8 fusion.65
  141.7 5.6 reduce-scatter.9.cloned.1.call-done
  147.3 2.6 all_gather.40
  153.0 60.8 %all-gather.6.cloned.1.call-done = bf16[768,1536]{1,0:T(8,128)(2,1)} async-done(((bf16[48,1536]{1,0:T(8,128)(2,1)}), bf16[768,1536]{1,0:T(8,128)(2,1)}) %all-gather.6.cloned.1.call-update) | async-done | bytes 2359312 | tf_op jit(solution)/shard_map/all_gather | solution.py:52
  213.8 6.0 convert_reduce_fusion
  222.6 4.1 fusion.57
  229.7 2.7 all_gather.44
  233.3 2.1 multiply_reduce_fusion.1
  236.0 5.3 reduce-scatter.11.cloned.1.call-done
  241.3 2.7 all_gather.43
  244.0 2.6 fusion.61
  252.7 2.0 fusion.9
  258.7 1.9 pad_maximum_fusion
  264.1 41.8 %reduce-scatter.15.cloned.1.call-done = f32[128,2,768]{0,2,1:T(8,128)} async-done(((f32[512,2,768]{0,2,1:T(8,128)}), f32[128,2,768]{0,2,1:T(8,128)}) %reduce-scatter.15.cloned.1.call-update) | async-done | bytes 786448 | tf_op jit(solution)/shard_map/reduce_scatter | solution.py:146
  307.5 3.1 convolution_bitcast_fusion.2
  310.7 2.5 convolution_bitcast_fusion
  313.1 6.2 copy.82
  321.9 3.2 fusion.55
  326.7 3.1 fusion.56
  332.1 2.7 all_gather.45
  335.6 79.0 %all-reduce.1 = (f32[768]{0:T(1024)}, f32[768]{0:T(1024)}, f32[2,384]{1,0:T(2,128)}, f32[768]{0:T(1024)}, f32[768]{0:T(1024)}, /*index=5*/f32[768]{0:T(1024)}, f32[1536]{0:T(1024)}, f32[768]{0:T(1024)}) all-reduce(f32[768]{0:T(1024)S(1)} %get-tuple-element.72, ...), channel_id=1, replica_groups=mesh['fsdp'=4,'ctx'=4,'tp'=2] {'fsdp','ctx'}, use_global_device_ids=true, to_apply=%region_17.18 | all-reduce | flops 6912 | bytes 55296 | tf_op jit(solution)/shard_map/psum | solution.py:185
  415.8 90.6 %all-reduce.4.cloned.1.call-done = f32[3,768,384]{2,0,1:T(4,128)} async-done(((f32[3,768,384]{2,0,1:T(4,128)}), f32[3,768,384]{2,0,1:T(4,128)}) %all-reduce.4.cloned.1.call-update) | async-done | bytes 3538960
  508.2 126.8 %reduce-scatter.19.cloned.1.call-done = f32[384,48]{0,1:T(8,128)} async-done(((f32[384,768]{0,1:T(8,128)}), f32[384,48]{0,1:T(8,128)}) %reduce-scatter.19.cloned.1.call-update) | async-done | bytes 73744 | tf_op jit(solution)/shard_map/reduce_scatter | solution.py:181
  634.9 143.1 %reduce-scatter.21.cloned.1.call-done = f32[48,1536]{1,0:T(8,128)} async-done(((f32[768,1536]{1,0:T(8,128)}), f32[48,1536]{1,0:T(8,128)}) %reduce-scatter.21.cloned.1.call-update) | async-done | bytes 294928 | tf_op jit(solution)/shard_map/reduce_scatter | solution.py:182
  778.0 142.2 %reduce-scatter.23.cloned.1.call-done = f32[1536,48]{0,1:T(8,128)} async-done(((f32[1536,768]{0,1:T(8,128)}), f32[1536,48]{0,1:T(8,128)}) %reduce-scatter.23.cloned.1.call-update) | async-done | bytes 294928 | tf_op jit(solution)/shard_map/reduce_scatter | solution.py:183
  (201 shorter events, 50.6 us)
Async XLA Ops:
  7.2 8.2 copy-start.34
  7.2 66.6 %all-gather.4.cloned.1.call-start = ((), (), s32[]{:S(2)}) async-start(), calls=%async_computation.8 | async-start | bytes 1880064 | tf_op jit(solution)/shard_map/all_gather | solution.py:50
  7.9 130.0 %all-gather.8.cloned.1.call-start = ((), (), s32[]{:S(2)}) async-start(), calls=%async_computation.11 | async-start | bytes 2506752 | tf_op jit(solution)/shard_map/all_gather | solution.py:53
  8.7 138.6 %reduce-scatter.9.cloned.1.call-start = ((), (), s32[]{:S(2)}) async-start(), calls=%async_computation.9 | async-start | bytes 1179648 | tf_op jit(solution)/shard_map/reduce_scatter | solution.py:19
  9.9 66.1 %copy-start.39 = (f32[256]{0:T(256)}, f32[256]{0:T(256)S(1)}, u32[]{:S(2)}) copy-start(f32[256]{0:T(256)S(1)} %get-tuple-element.100) | copy-start | bytes 3076
  10.7 90.8 %copy-start.32 = (f32[6,64]{1,0:T(8,128)}, f32[6,64]{1,0:T(8,128)S(1)}, u32[]{:S(2)}) copy-start(f32[6,64]{1,0:T(8,128)S(1)} %add.169) | copy-start | bytes 4612
  12.5 63.4 %copy-start.43 = (f32[256]{0:T(256)}, f32[256]{0:T(256)S(1)}, u32[]{:S(2)}) copy-start(f32[256]{0:T(256)S(1)} %bitcast_rsqrt_fusion) | copy-start | bytes 3076
  15.4 60.6 %copy-start.14 = (bf16[256,768]{1,0:T(8,128)(2,1)}, bf16[256,768]{1,0:T(8,128)(2,1)S(1)}, u32[]{:S(2)}) copy-start(bf16[256,768]{1,0:T(8,128)(2,1)S(1)} %fusion.22) | copy-start | bytes 1179652
  76.5 25.0 %copy-start.16 = (f32[2,128,6,64]{1,0,3,2:T(2,128)}, f32[2,128,6,64]{1,0,3,2:T(2,128)S(1)}, u32[]{:S(2)}) copy-start(f32[2,128,6,64]{1,0,3,2:T(2,128)S(1)} %squeeze.8) | copy-start | bytes 1179652
  106.8 31.1 %copy-start.22 = (bf16[2,128,6,64]{1,0,3,2:T(2,128)(2,1)}, bf16[2,128,6,64]{1,0,3,2:T(2,128)(2,1)S(1)}, u32[]{:S(2)}) copy-start(bf16[2,128,6,64]{1,0,3,2:T(2,128)(2,1)S(1)} %copy.73) | copy-start | bytes 589828
  108.2 105.7 %all-gather.6.cloned.1.call-start = ((), (), s32[]{:S(2)}) async-start(), calls=%async_computation.10 | async-start | bytes 2506752 | tf_op jit(solution)/shard_map/all_gather | solution.py:52
  108.7 121.0 %reduce-scatter.13.cloned.1.call-start = ((), (), s32[]{:S(2)}) async-start(), calls=%async_computation.13 | async-start | bytes 1179648 | tf_op jit(solution)/shard_map/reduce_scatter | solution.py:19
  138.0 11.9 %copy-start.2 = (bf16[2,128,768]{2,1,0:T(8,128)(2,1)S(1)}, bf16[2,128,768]{2,1,0:T(8,128)(2,1)}, u32[]{:S(2)}) copy-start(bf16[2,128,768]{2,1,0:T(8,128)(2,1)} %param.15) | copy-start | bytes 1179652
  141.7 72.1 %copy-start.29 = (f32[768]{0:T(1024)S(1)}, f32[768]{0:T(1024)}, u32[]{:S(2)}) copy-start(f32[768]{0:T(1024)} %param.23) | copy-start | bytes 9220
  141.7 72.1 %copy-start.30 = (f32[768]{0:T(1024)S(1)}, f32[768]{0:T(1024)}, u32[]{:S(2)}) copy-start(f32[768]{0:T(1024)} %param.24) | copy-start | bytes 9220
  213.8 6.9 copy-start.56
  222.5 18.8 %reduce-scatter.11.cloned.1.call-start = ((), (), s32[]{:S(2)}) async-start(), calls=%async_computation.12 | async-start | bytes 1179648 | tf_op jit(solution)/shard_map/reduce_scatter | solution.py:19
  226.7 79.2 %reduce-scatter.15.cloned.1.call-start = ((), (), s32[]{:S(2)}) async-start(), calls=%async_computation.14 | async-start | bytes 3932160 | tf_op jit(solution)/shard_map/reduce_scatter | solution.py:146
  228.0 16.0 %copy-start.36 = (f32[256]{0:T(256)S(1)}, f32[256]{0:T(256)}, u32[]{:S(2)}) copy-start(f32[256]{0:T(256)} %copy-done.35) | copy-start | bytes 3076
  228.0 16.0 %copy-start.41 = (f32[256]{0:T(256)S(1)}, f32[256]{0:T(256)}, u32[]{:S(2)}) copy-start(f32[256]{0:T(256)} %fusion.44) | copy-start | bytes 3076
  229.7 5.7 copy-start.52
  246.6 6.1 copy-start.53
  260.6 71.4 %reduce-scatter.17.cloned.1.call-start = ((), (), s32[]{:S(2)}) async-start(), calls=%async_computation.15 | async-start | bytes 1179648 | tf_op jit(solution)/shard_map/reduce_scatter | solution.py:19
  310.6 195.8 %all-reduce.4.cloned.1.call-start = ((), (), s32[]{:S(2)}) async-start(), calls=%async_computation.19 | async-start | bytes 9437184
  319.4 315.5 %reduce-scatter.19.cloned.1.call-start = ((), (), s32[]{:S(2)}) async-start(), calls=%async_computation.16 | async-start | bytes 1253376 | tf_op jit(solution)/shard_map/reduce_scatter | solution.py:181
  321.9 456.1 %reduce-scatter.21.cloned.1.call-start = ((), (), s32[]{:S(2)}) async-start(), calls=%async_computation.17 | async-start | bytes 5013504 | tf_op jit(solution)/shard_map/reduce_scatter | solution.py:182
  325.2 595.0 %reduce-scatter.23.cloned.1.call-start = ((), (), s32[]{:S(2)}) async-start(), calls=%async_computation.18 | async-start | bytes 5013504 | tf_op jit(solution)/shard_map/reduce_scatter | solution.py:183
  329.8 5.0 copy-start.31
  329.8 5.3 copy-start.50
  329.8 5.3 copy-start.44
  332.0 82.5 %copy-start.9 = (f32[256,768]{1,0:T(8,128)S(1)}, f32[256,768]{1,0:T(8,128)}, u32[]{:S(2)}) copy-start(f32[256,768]{1,0:T(8,128)} %copy-done.8) | copy-start | bytes 2359300
  332.0 82.5 %copy-start.54 = (f32[256]{0:T(256)S(1)}, f32[256]{0:T(256)}, u32[]{:S(2)}) copy-start(f32[256]{0:T(256)} %copy-done.53) | copy-start | bytes 3076
  (38 other events, 71.4 us)
Sparse Core Ops, SparseCore 0:
  10.7 63.0 all-gather.3
  76.6 61.3 all-gather.7
  140.2 7.0 reduce-scatter.8
  150.3 63.4 all-gather.5
  222.6 7.0 reduce-scatter.12
  231.8 9.4 reduce-scatter.10
  260.8 45.0 reduce-scatter.14
  310.7 8.2 reduce-scatter.16
  324.8 181.6 all-reduce.3
  512.4 122.5 reduce-scatter.18
  641.5 136.4 reduce-scatter.20
  783.6 136.5 reduce-scatter.22
where the time goes:
time: 928 us; the launch traced here: 927 us
  waiting for transfers between devices  658 us (71%)
  blocking collectives  162 us (17%)
  matrix products  42.2 us (5%)
  local copies, waits for them, and re-layouts  27.4 us (3%)
  other arithmetic  21.6 us (2%)
  between operations  15.6 us (2%)
    reduce_scatter x1, waiting for transfers between devices, body(): lax.psum_scatter(grad_upweight, ('fsdp', 'ctx'), scatter_dimension=0, til...  143 us
    reduce_scatter x1, waiting for transfers between devices, body(): lax.psum_scatter(grad_downweight, ('fsdp', 'ctx'), scatter_dimension=1, t...  142 us
    reduce_scatter x1, waiting for transfers between devices, body(): lax.psum_scatter(grad_outweight, ('fsdp', 'ctx'), scatter_dimension=1, ti...  127 us
    unnamed x13, waiting for transfers between devices  92.7 us
    psum x1, blocking collectives, body(): lax.psum((grad_firstgain, grad_firstshift, grad_qvbias, grad_outbias, gra...  79 us
    all_gather x1, waiting for transfers between devices, body(): lax.all_gather(up_weight, ('fsdp', 'ctx'), axis=0, tiled=True)  60.8 us
    all_gather x1, blocking collectives, body(): lax.all_gather(out_weight, ('fsdp', 'ctx'), axis=1, tiled=True)  49.5 us
    reduce_scatter x1, waiting for transfers between devices, body(): lax.psum_scatter(jnp.concatenate((key_part.reshape(amount, seq_count, loc...  41.8 us
  transfers between devices with their start and end apart: 12, of which 11 were waited for; matrix products, arithmetic and copies ran while one was open for 6% of the time, Pallas kernels for 0%

commit v1 on v0

v1 whole, which is shorter than its diff:
```python
import functools
import math

import jax
import jax.numpy as jnp
from jax import lax
from jax.experimental import pallas as pl
from jax.experimental.pallas import tpu as pltpu
from jax.sharding import PartitionSpec as P

HEAD = 64
MESH = pl.DeviceIdType.MESH


def partners(z_peers):
    me_c = lax.axis_index("ctx")
    side = me_c + 1 - 2 * (me_c % 2)
    over = (me_c + 2) % 4
    me_f = lax.axis_index("fsdp")
    count = lax.axis_size("fsdp")
    peers = [(me_f + t) % count for t in range(1, count)] if z_peers else []
    return me_c, side, over, 3 - me_c, me_f, peers


def greet(side, over, peers):
    barrier = pltpu.get_barrier_semaphore()
    for target in (side, over):
        pl.semaphore_signal(barrier, inc=1, device_id={"ctx": target}, device_id_type=MESH)
    for target in peers:
        pl.semaphore_signal(barrier, inc=1, device_id={"fsdp": target}, device_id_type=MESH)
    pl.semaphore_wait(barrier, 2 + len(peers))


def remote(src, dst, send, recv, axis, target):
    return pltpu.make_async_remote_copy(
        src_ref=src, dst_ref=dst, send_sem=send, recv_sem=recv,
        device_id={axis: target}, device_id_type=MESH,
    )


def gather_kernel(arrays, slots, z_peers, *refs):
    ins, outs = refs[:arrays], refs[arrays : 2 * arrays]
    z_send, z_recv, xy_send, xy_recv = refs[2 * arrays :]
    me_c, side, over, _, me_f, peers = partners(z_peers)
    greet(side, over, peers)
    started = []

    def go(copy):
        copy.start()
        started.append(copy)

    def slot(s):
        return (me_f + s) % slots if z_peers else s

    def own(k, s):
        if z_peers and s > 0:
            return outs[k].at[slot(s), me_c]
        return ins[k].at[0 if z_peers else s]

    nearest = sorted(range(slots), key=lambda s: min(s, slots - s))
    if z_peers:
        for k in range(arrays):
            for t in nearest[1:]:
                go(remote(ins[k].at[0], outs[k].at[me_f, me_c], z_send.at[k, t], z_recv.at[k, slots - t], "fsdp", peers[t - 1]))
        order = [(k, 0) for k in range(arrays)]
        order += [(k, s) for k in range(arrays) for s in nearest[1:]]
    else:
        order = [(k, s) for k in range(arrays) for s in range(slots)]

    def forward(k, s):
        src = own(k, s)
        if z_peers and s > 0:
            remote(src, src, z_send.at[k, s], z_recv.at[k, s], "fsdp", peers[0]).wait_recv()
        dst = outs[k].at[slot(s), me_c]
        go(remote(src, dst, xy_send.at[0, k, s], xy_recv.at[0, k, s], "ctx", side))
        go(remote(src, dst, xy_send.at[1, k, s], xy_recv.at[1, k, s], "ctx", over))

    def arrived(way, k, s, from_c):
        ref = outs[k].at[slot(s), from_c]
        remote(ref, ref, xy_send.at[way, k, s], xy_recv.at[way, k, s], "ctx", side).wait_recv()
        return ref

    def relay(k, s):
        if (k + s) % 2 == 0:
            ref = arrived(0, k, s, side)
            go(remote(ref, ref, xy_send.at[2, k, s], xy_recv.at[2, k, s], "ctx", over))
        else:
            ref = arrived(1, k, s, over)
            go(remote(ref, ref, xy_send.at[2, k, s], xy_recv.at[2, k, s], "ctx", side))

    lag = 2 if len(order) > 4 else len(order)
    for at, (k, s) in enumerate(order):
        forward(k, s)
        if at >= lag:
            relay(*order[at - lag])
    for k in range(arrays):
        if z_peers:
            outs[k][me_f, me_c] = ins[k][0]
        else:
            for s in range(slots):
                outs[k][s, me_c] = ins[k][s]
    for k, s in order[len(order) - lag :]:
        relay(k, s)
    for k, s in order:
        if (k + s) % 2 == 0:
            arrived(1, k, s, over)
        else:
            arrived(0, k, s, side)
        arrived(2, k, s, 3 - me_c)
    for copy in started:
        copy.wait_send()


def gather_blocks(shards, slots, z_peers, collective_id):
    arrays = len(shards)
    spec = pl.BlockSpec(memory_space=pltpu.VMEM)
    size = sum(x.size * 2 for x in shards) * 4 * (slots if z_peers else 1)
    return pl.pallas_call(
        functools.partial(gather_kernel, arrays, slots, z_peers),
        out_shape=[jax.ShapeDtypeStruct((slots, 4) + x.shape[1:], x.dtype) for x in shards],
        in_specs=[spec] * arrays,
        out_specs=[spec] * arrays,
        scratch_shapes=[
            pltpu.SemaphoreType.DMA((arrays, slots)),
            pltpu.SemaphoreType.DMA((arrays, slots)),
            pltpu.SemaphoreType.DMA((3, arrays, slots)),
            pltpu.SemaphoreType.DMA((3, arrays, slots)),
        ],
        compiler_params=pltpu.CompilerParams(
            collective_id=collective_id, has_side_effects=True, vmem_limit_bytes=int(size * 1.25) + (4 << 20)
        ),
        cost_estimate=pl.CostEstimate(flops=0, bytes_accessed=2 * size, transcendentals=0),
    )(*shards)


def scatter_kernel(arrays, slots, z_peers, *refs):
    ins, outs = refs[:arrays], refs[arrays : 2 * arrays]
    per = refs[2 * arrays :]
    first, mixed, second = per[:arrays], per[arrays : 2 * arrays], per[2 * arrays : 3 * arrays]
    rest = per[3 * arrays :]
    if z_peers:
        z_out, z_in = rest[:arrays], rest[arrays : 2 * arrays]
        rest = rest[2 * arrays :]
    a_send, a_recv, b_send, b_recv, z_send, z_recv = rest
    me_c, side, over, across, me_f, peers = partners(z_peers)
    greet(side, over, peers)
    f32 = jnp.float32
    started = []

    def go(copy):
        copy.start()
        started.append(copy)

    def slot(s):
        return (me_f + s) % slots if z_peers else s

    far = sorted(range(slots), key=lambda s: -min(s, slots - s))
    order = [(k, s) for k in range(arrays) for s in far]

    def ways(k, s):
        return (side, over) if (k + s) % 2 == 0 else (over, side)

    for k, s in order:
        near, other = ways(k, s)
        go(remote(ins[k].at[slot(s), across], first[k].at[s, 1], a_send.at[1, k, s], a_recv.at[1, k, s], "ctx", near))
        go(remote(ins[k].at[slot(s), near], first[k].at[s, 0], a_send.at[0, k, s], a_recv.at[0, k, s], "ctx", near))

    def middle(k, s):
        near, other = ways(k, s)
        landed = first[k].at[s, 1]
        remote(landed, landed, a_send.at[1, k, s], a_recv.at[1, k, s], "ctx", near).wait_recv()
        mixed[k][s] = (ins[k][slot(s), other].astype(f32) + landed[...].astype(f32)).astype(jnp.bfloat16)
        go(remote(mixed[k].at[s], second[k].at[s], b_send.at[k, s], b_recv.at[k, s], "ctx", other))

    def last(k, s):
        near, other = ways(k, s)
        landed = first[k].at[s, 0]
        remote(landed, landed, a_send.at[0, k, s], a_recv.at[0, k, s], "ctx", near).wait_recv()
        more = second[k].at[s]
        remote(more, more, b_send.at[k, s], b_recv.at[k, s], "ctx", other).wait_recv()
        total = ins[k][slot(s), me_c].astype(f32) + landed[...].astype(f32) + more[...].astype(f32)
        if not z_peers:
            outs[k][s] = total
        elif s == 0:
            outs[k][0] = total
        else:
            z_out[k][s] = total.astype(jnp.bfloat16)
            go(remote(z_out[k].at[s], z_in[k].at[slots - s], z_send.at[k, s], z_recv.at[k, slots - s], "fsdp", peers[s - 1]))

    lag = 3 if len(order) > 4 else len(order)
    for at, (k, s) in enumerate(order):
        middle(k, s)
        if at >= lag:
            last(*order[at - lag])
    for k, s in order[len(order) - lag :]:
        last(k, s)
    if z_peers:
        for k in range(arrays):
            total = outs[k][0]
            for s in range(1, slots):
                ref = z_in[k].at[s]
                remote(ref, ref, z_send.at[k, s], z_recv.at[k, s], "fsdp", peers[0]).wait_recv()
                total = total + ref[...].astype(f32)
            outs[k][0] = total
    for copy in started:
        copy.wait_send()


def scatter_blocks(parts, z_peers, collective_id):
    arrays = len(parts)
    slots = parts[0].shape[0]
    bf16 = jnp.bfloat16
    spec = pl.BlockSpec(memory_space=pltpu.VMEM)
    dims = [x.shape[2:] for x in parts]
    scratch = [pltpu.VMEM((slots, 2) + d, bf16) for d in dims]
    scratch += [pltpu.VMEM((slots,) + d, bf16) for d in dims] * 2
    if z_peers:
        scratch += [pltpu.VMEM((slots,) + d, bf16) for d in dims] * 2
    scratch += [pltpu.SemaphoreType.DMA((2, arrays, slots))] * 2
    scratch += [pltpu.SemaphoreType.DMA((arrays, slots))] * 4
    size = sum(x.size * 2 for x in parts)
    return pl.pallas_call(
        functools.partial(scatter_kernel, arrays, slots, z_peers),
        out_shape=[jax.ShapeDtypeStruct((1 if z_peers else slots,) + d, jnp.float32) for d in dims],
        in_specs=[spec] * arrays,
        out_specs=[spec] * arrays,
        scratch_shapes=scratch,
        compiler_params=pltpu.CompilerParams(
            collective_id=collective_id, has_side_effects=True, vmem_limit_bytes=int(size * 3) + (6 << 20)
        ),
        cost_estimate=pl.CostEstimate(flops=0, bytes_accessed=2 * size, transcendentals=0),
    )(*parts)


def norm_rows(rows_in, row_gain, row_shift):
    centre_mean = jnp.mean(rows_in, axis=-1, keepdims=True)
    centred = rows_in - centre_mean
    variance = jnp.mean(centred * centred, axis=-1, keepdims=True)
    return centred * lax.rsqrt(variance + 1e-05) * row_gain + row_shift


def head_sum(pieces):
    count = lax.axis_size("tp")
    total = pieces
    moved = pieces
    for _ in range(count - 1):
        moved = lax.ppermute(moved, "tp", [(i, (i + 1) % count) for i in range(count)])
        total = total + moved
    return total


def sum_small(arrays):
    sizes = [x.size for x in arrays]
    packed = jnp.concatenate([x.reshape(-1) for x in arrays]).reshape(-1, 128)
    for axis in ("ctx", "fsdp"):
        count = lax.axis_size(axis)
        bit = 1
        while bit < count:
            packed = packed + lax.ppermute(packed, axis, [(i, i ^ bit) for i in range(count)])
            bit *= 2
    flat = packed.reshape(-1)
    result, at = [], 0
    for x, size in zip(arrays, sizes):
        result.append(flat[at : at + size].reshape(x.shape))
        at += size
    return result


def gather_weights(shards):
    if lax.axis_size("fsdp") <= 4:
        full = gather_blocks([x[None] for x in shards], lax.axis_size("fsdp"), True, 1)
        return [x.reshape(-1, x.shape[-1]) for x in full]
    return [lax.all_gather(x, ("fsdp", "ctx"), axis=0, tiled=True) for x in shards]


def scatter_weights(parts):
    slots = lax.axis_size("fsdp")
    if slots <= 4:
        blocks = [x.astype(jnp.bfloat16).reshape(slots, 4, -1, x.shape[-1]) for x in parts]
        return [x[0] for x in scatter_blocks(blocks, True, 2)]
    return [lax.psum_scatter(x, ("fsdp", "ctx"), scatter_dimension=0, tiled=True) for x in parts]


def body(
    layer_input,
    lengths,
    first_gain,
    first_shift,
    qkv_weight,
    qv_bias,
    out_weight,
    out_bias,
    second_gain,
    second_shift,
    up_weight,
    up_bias,
    down_weight,
    down_bias,
    cotangent,
):
    seq_count, span, width = layer_input.shape
    row_count = seq_count * span
    local_width = qkv_weight.shape[2]
    head_count = local_width // HEAD
    full_length = span * lax.axis_size("ctx")
    score_scale = 1.0 / math.sqrt(HEAD)
    f32 = jnp.float32
    bf16 = jnp.bfloat16
    inputs = layer_input.astype(f32).reshape(row_count, width)
    first_shard = jnp.concatenate([qkv_weight[0], qkv_weight[1], qkv_weight[2], out_weight.T], axis=1)
    first_full, up_full, down_full = gather_weights([first_shard, up_weight, down_weight.T])
    qkv_full = first_full[:, : 3 * local_width]
    out_full = first_full[:, 3 * local_width :]
    normed_low = norm_rows(inputs, first_gain, first_shift).astype(bf16)
    projected = jnp.dot(normed_low, qkv_full, preferred_element_type=f32)
    queries = (projected[:, :local_width] + qv_bias[0]).astype(bf16)
    key_local = projected[:, local_width : 2 * local_width].astype(bf16)
    value_local = (projected[:, 2 * local_width :] + qv_bias[1]).astype(bf16)
    key_all, value_all = gather_blocks(
        [x.reshape(seq_count, span, local_width) for x in (key_local, value_local)], seq_count, False, 3
    )
    query_heads = queries.reshape(seq_count, span, head_count, HEAD)
    query_pos = lax.axis_index("ctx") * span + jnp.arange(span, dtype=jnp.int32)
    key_pos = jnp.arange(full_length, dtype=jnp.int32)
    allowed = (key_pos[None, :] <= query_pos[:, None])[None, None] & (
        key_pos[None, None, None, :] < lengths[:, None, None, None]
    )

    def masked_scores(key_source):
        key_heads = key_source.reshape(seq_count, full_length, head_count, HEAD)
        scores = (
            jnp.einsum("suhe,snhe->shun", query_heads, key_heads, preferred_element_type=f32)
            * score_scale
        )
        return jnp.where(allowed, scores, -1e30)

    masked = masked_scores(key_all)
    peak = jnp.max(masked, axis=-1, keepdims=True)
    expo = jnp.where(allowed, jnp.exp(masked - peak), 0.0)
    row_total = jnp.sum(expo, axis=-1, keepdims=True)
    probs = expo / row_total
    probs_low = probs.astype(bf16)
    value_heads = value_all.reshape(seq_count, full_length, head_count, HEAD)
    attended = jnp.einsum("shun,snhe->suhe", probs_low, value_heads, preferred_element_type=f32)
    attended = attended.reshape(row_count, local_width).astype(bf16)
    residual = inputs + head_sum(jnp.einsum("rc,dc->rd", attended, out_full, preferred_element_type=f32)) + out_bias
    normed_two_low = norm_rows(residual, second_gain, second_shift).astype(bf16)
    up_proj = jnp.dot(normed_two_low, up_full, preferred_element_type=f32) + up_bias
    activated_low = jax.nn.gelu(up_proj, approximate=True).astype(bf16)
    mixed = head_sum(jnp.einsum("rf,df->rd", activated_low, down_full, preferred_element_type=f32))
    layer_output = (residual + mixed + down_bias).astype(bf16).reshape(seq_count, span, width)
    grad_out = cotangent.reshape(row_count, width)
    grad_downbias = jnp.sum(grad_out.astype(f32), axis=0)
    grad_downweight = jnp.einsum("rd,rf->df", grad_out, activated_low, preferred_element_type=f32)
    grad_act = jnp.einsum("rd,df->rf", grad_out, down_full, preferred_element_type=f32)
    gelu_back = jax.vjp(lambda z: jax.nn.gelu(z, approximate=True), up_proj)[1]
    grad_up = gelu_back(grad_act)[0].astype(bf16)
    grad_upbias = jnp.sum(grad_up.astype(f32), axis=0)
    grad_upweight = jnp.einsum("rd,rf->df", normed_two_low, grad_up, preferred_element_type=f32)
    grad_normtwo = head_sum(jnp.einsum("rf,df->rd", grad_up, up_full, preferred_element_type=f32))
    second_back = jax.vjp(norm_rows, residual, second_gain, second_shift)[1]
    grad_resid_norm, grad_secondgain, grad_secondshift = second_back(grad_normtwo)
    grad_residual = grad_out.astype(f32) + grad_resid_norm
    grad_branch = grad_residual.astype(bf16)
    grad_outbias = jnp.sum(grad_branch.astype(f32), axis=0)
    grad_outweight = jnp.einsum("rd,rc->dc", grad_branch, attended, preferred_element_type=f32)
    grad_attended = jnp.einsum(
        "rd,dc->rc", grad_branch, out_full, preferred_element_type=f32
    ).astype(bf16)
    probs_again = probs
    probs_low_again = probs_low
    key_heads_back = key_all.reshape(seq_count, full_length, head_count, HEAD)
    value_heads_back = value_all.reshape(seq_count, full_length, head_count, HEAD)
    grad_att_heads = grad_attended.reshape(seq_count, span, head_count, HEAD)
    grad_probs = jnp.einsum(
        "suhe,snhe->shun", grad_att_heads, value_heads_back, preferred_element_type=f32
    )
    inner_total = jnp.sum(probs_again * grad_probs, axis=-1, keepdims=True)
    grad_scores = (probs_again * (grad_probs - inner_total)).astype(bf16)
    grad_query = (
        jnp.einsum("shun,snhe->suhe", grad_scores, key_heads_back, preferred_element_type=f32)
        * score_scale
    )
    grad_query = grad_query.astype(bf16).reshape(row_count, local_width)
    key_part = (
        jnp.einsum("shun,suhe->snhe", grad_scores, query_heads, preferred_element_type=f32)
        * score_scale
    )
    value_part = jnp.einsum(
        "shun,suhe->snhe", probs_low_again, grad_att_heads, preferred_element_type=f32
    )
    key_grads, value_grads = scatter_blocks(
        [x.astype(bf16).reshape(seq_count, 4, span, local_width) for x in (key_part, value_part)], False, 4
    )
    grad_key = key_grads.astype(bf16).reshape(row_count, local_width)
    grad_value = value_grads.astype(bf16).reshape(row_count, local_width)
    grad_proj = jnp.concatenate((grad_query, grad_key, grad_value), axis=1)
    grad_qvbias = jnp.stack(
        (jnp.sum(grad_query.astype(f32), axis=0), jnp.sum(grad_value.astype(f32), axis=0))
    )
    grad_first = jnp.concatenate(
        (jnp.einsum("rd,rc->dc", normed_low, grad_proj, preferred_element_type=f32), grad_outweight), axis=1
    )
    grad_normed = head_sum(jnp.einsum("rc,dc->rd", grad_proj, qkv_full, preferred_element_type=f32))
    first_back = jax.vjp(norm_rows, inputs, first_gain, first_shift)[1]
    grad_in_norm, grad_firstgain, grad_firstshift = first_back(grad_normed)
    grad_input = (grad_residual + grad_in_norm).reshape(seq_count, span, width)
    first_sum, up_sum, down_sum = scatter_weights([grad_first, grad_upweight, grad_downweight])
    weight_grads = (
        jnp.stack([first_sum[:, k * local_width : (k + 1) * local_width] for k in range(3)]),
        first_sum[:, 3 * local_width :].T,
        up_sum,
        down_sum.T,
    )
    small_sums = sum_small(
        (
            grad_firstgain,
            grad_firstshift,
            grad_qvbias,
            grad_outbias,
            grad_secondgain,
            grad_secondshift,
            grad_upbias,
            grad_downbias,
        )
    )
    return (
        layer_output,
        grad_input,
        small_sums[0],
        small_sums[1],
        weight_grads[0],
        small_sums[2],
        weight_grads[1],
        small_sums[3],
        small_sums[4],
        small_sums[5],
        weight_grads[2],
        small_sums[6],
        weight_grads[3],
        small_sums[7],
    )


def solution(mesh):
    in_specs = (
        P("fsdp", "ctx", None),
        P("fsdp"),
        P(),
        P(),
        P(None, ("fsdp", "ctx"), "tp"),
        P(None, "tp"),
        P("tp", ("fsdp", "ctx")),
        P(),
        P(),
        P(),
        P(("fsdp", "ctx"), "tp"),
        P("tp"),
        P("tp", ("fsdp", "ctx")),
        P(),
        P("fsdp", "ctx", None),
    )
    out_specs = (
        P("fsdp", "ctx", None),
        P("fsdp", "ctx", None),
        P(),
        P(),
        P(None, ("fsdp", "ctx"), "tp"),
        P(None, "tp"),
        P("tp", ("fsdp", "ctx")),
        P(),
        P(),
        P(),
        P(("fsdp", "ctx"), "tp"),
        P("tp"),
        P("tp", ("fsdp", "ctx")),
        P(),
    )
    return jax.shard_map(body, mesh=mesh, in_specs=in_specs, out_specs=out_specs, check_vma=False)
```

time: 928 us -> 280 us (0.30)
  waiting for transfers between devices: 658 us -> 6.5 us
  Pallas kernels: 0 us -> 182 us
  blocking collectives: 162 us -> 0 us
  between operations: 15.6 us -> 1.48 us
  matrix products: 42.2 us -> 32.4 us
  starting transfers between devices: 0.49 us -> 9.99 us
    reduce_scatter x8 -> x0, waiting for transfers between devices: 466 us -> none  [the longest x1 143 us: body(): lax.psum_scatter(grad_upweight, ('fsdp', 'ctx'), scatter_dimension=0, til...]
    pallas_call x0 -> x4, Pallas kernels: none -> 182 us  [the longest x2 100 us: scatter_blocks(): pl.pallas_call(functools.partial(scatter_kernel, arrays, slots, z_peers),...]
    all_gather x3 -> x0, waiting for transfers between devices: 98.9 us -> none  [the longest x1 60.8 us: body(): lax.all_gather(up_weight, ('fsdp', 'ctx'), axis=0, tiled=True)]
    unnamed x13 -> x0, waiting for transfers between devices: 92.7 us -> none
    all_gather x7 -> x0, blocking collectives: 82.8 us -> none  [the longest x1 49.5 us: body(): lax.all_gather(out_weight, ('fsdp', 'ctx'), axis=1, tiled=True)]
    psum x1 -> x0, blocking collectives: 79 us -> none  [body(): lax.psum((grad_firstgain, grad_firstshift, grad_qvbias, grad_outbias, gra...]
    reshape x0 -> x10, local copies, waits for them, and re-layouts: none -> 11.5 us  [the longest x4 8.6 us: body(): x.astype(bf16).reshape(seq_count, 4, span, local_width)]
    ppermute x0 -> x8, starting transfers between devices: none -> 9.99 us  [the longest x4 9.27 us: sum_small(): lax.ppermute(packed, axis, [(i, i ^ bit) for i in range(count)])]
  transfers between devices with their start and end apart: 12 -> 8, of which waited for: 11 -> 5; matrix products, arithmetic and copies ran while one was open for 6% -> 5% of each run, Pallas kernels for 0% -> 30%
where the time goes in v1:
time: 280 us; the launch traced here: 279 us
  Pallas kernels  182 us (65%)
  local copies, waits for them, and re-layouts  32.9 us (12%)
  matrix products  32.4 us (12%)
  other arithmetic  14.4 us (5%)
  starting transfers between devices  9.99 us (4%)
  waiting for transfers between devices  6.5 us (2%)
    pallas_call x2, Pallas kernels, scatter_blocks(): pl.pallas_call(functools.partial(scatter_kernel, arrays, slots, z_peers),...  100 us
    pallas_call x2, Pallas kernels, gather_blocks(): pl.pallas_call(functools.partial(gather_kernel, arrays, slots, z_peers),...  81.3 us
    unnamed x110, local copies, waits for them, and re-layouts  10.6 us
    ppermute x4, starting transfers between devices, sum_small(): lax.ppermute(packed, axis, [(i, i ^ bit) for i in range(count)])  9.27 us
    reshape x4, local copies, waits for them, and re-layouts, body(): x.astype(bf16).reshape(seq_count, 4, span, local_width)  8.6 us
  transfers between devices with their start and end apart: 8, of which 5 were waited for; matrix products, arithmetic and copies ran while one was open for 5% of the time, Pallas kernels for 30%

profile of v1, /device:TPU:0, one launch (start us, length us, event | category | flops | bytes accessed | tf_op | source)
XLA Modules:
  0.0 279.2 jit_solution(3550286822810352534)
XLA Ops:
  6.6 64.8 %shard_map.254 = (bf16[4,4,48,1536]{3,2,1,0:T(8,128)(2,1)S(1)}, bf16[4,4,48,1536]{3,2,1,0:T(8,128)(2,1)S(1)}, bf16[4,4,48,1536]{3,2,1,0:T(8,128)(2,1)S(1)}) custom-call(bf16[1,48,1536]{2,1,0:T(8,128)(2,1)S(1)} %maximum_bitcast_fusion.refs_0_, bf16[1,48,1536]{2,1,0:T(8,128)(2,1)S(1)} %bitcast.186, bf16[1,48,1536]{2,1,0:T(8,128)(2,1)S(1)} %bitcast.187), custom_call_target="tpu_custom_call" | custom-call | bytes 14155776 | tf_op jit(solution)/shard_map/pallas_call | solution.py:118
  71.4 1.4 copy-done.5
  72.8 1.5 copy-done.7
  75.3 16.5 %shard_map.255 = (bf16[2,4,128,384]{3,2,1,0:T(8,128)(2,1)S(1)}, bf16[2,4,128,384]{3,2,1,0:T(8,128)(2,1)S(1)}) custom-call(bf16[2,128,384]{2,1,0:T(8,128)(2,1)S(1)} %bitcast.178, bf16[2,128,384]{2,1,0:T(8,128)(2,1)S(1)} %bitcast.177), custom_call_target="tpu_custom_call" | custom-call | bytes 3145728 | tf_op jit(solution)/shard_map/pallas_call | solution.py:118
  95.2 3.1 %fusion.71 = (f32[2,6,128]{2,1,0:T(8,128)S(1)}, f32[2,6,128,512]{3,2,1,0:T(8,128)}) fusion(pred[2,128,512]{2,1,0:T(8,128)(4,1)S(1)} %broadcast_and_fusion, bf16[2,512,6,64]{1,3,2,0:T(8,128)(2,1)S(1)} %reshape.264, bf16[2,128,6,64]{1,0,3,2:T(2,128)(2,1)S(1)} %reshape.263), kind=kOutput, calls=%fused_computation.150 | convolution fusion | flops 104595968 | bytes 4265984 | tf_op jit(solution)/shard_map/sub | solution.py:339
  98.3 2.6 fusion.19
  101.2 1.5 fusion.37
  107.3 2.0 convert_reduce_fusion
  111.8 2.4 convolution_convert_fusion
  118.9 2.1 convolution_convert_fusion.6
  121.0 1.7 copy.46
  122.7 1.7 reshape.269
  124.4 3.1 %multiply_reduce_fusion = (f32[2,6,128]{2,1,0:T(8,128)S(1)}, f32[2,6,128,512]{3,2,1,0:T(8,128)S(1)}) fusion(f32[2,6,128,512]{3,2,1,0:T(8,128)} %get-tuple-element.73, f32[2,6,128]{2,1,0:T(8,128)} %copy-done.41, bf16[2,512,6,64]{1,3,2,0:T(8,128)(2,1)} %reshape.262, bf16[2,128,6,64]{1,0,3,2:T(2,128)(2,1)} %reshape.269), kind=kOutput, calls=%fused_computation.5 | convolution fusion | flops 103021056 | bytes 7286784 | tf_op jit(solution)/shard_map/suhe,snhe->shun/dot_general | solution.py:375
  127.6 1.4 fusion.17
  131.2 1.9 convert_reduce_fusion.5
  133.1 2.4 reshape.271
  135.5 1.5 copy.51.refs_0_
  137.1 2.4 reshape.272
  139.5 2.2 copy.52.refs_1_
  142.8 16.0 %shard_map.256 = (f32[2,128,384]{2,1,0:T(8,128)S(1)}, f32[2,128,384]{2,1,0:T(8,128)S(1)}) custom-call(bf16[2,4,128,384]{3,2,1,0:T(8,128)(2,1)S(1)} %copy.51.refs_0_, bf16[2,4,128,384]{3,2,1,0:T(8,128)(2,1)S(1)} %copy-done), custom_call_target="tpu_custom_call" | custom-call | bytes 3145728 | tf_op jit(solution)/shard_map/pallas_call | solution.py:222
  161.3 3.4 %fusion.12 = f32[256,768]{1,0:T(8,128)} fusion(bf16[768,1536]{1,0:T(8,128)(2,1)} %bitcast.185, bf16[256,384]{1,0:T(8,128)(2,1)} %bitcast.204, bf16[256,384]{1,0:T(8,128)(2,1)} %bitcast.206, bf16[256,384]{1,0:T(8,128)(2,1)S(1)} %copy.53), kind=kOutput, calls=%fused_computation.28 | convolution fusion | flops 454754304 | bytes 3145728 | tf_op jit(solution)/shard_map/rc,dc->rd/dot_general | solution.py:404
  167.0 1.4 convolution_convert_fusion.4
  168.4 1.9 convolution_convert_fusion.2
  170.5 1.4 copy-done.1
  171.9 84.3 %shard_map.257 = (f32[1,48,1536]{2,1,0:T(8,128)S(1)}, f32[1,48,1536]{2,1,0:T(8,128)S(1)}, f32[1,48,1536]{2,1,0:T(8,128)S(1)}) custom-call(bf16[4,4,48,1536]{3,2,1,0:T(8,128)(2,1)S(1)} %pad_maximum_fusion.refs_0_, bf16[4,4,48,1536]{3,2,1,0:T(8,128)(2,1)S(1)} %bitcast.175, bf16[4,4,48,1536]{3,2,1,0:T(8,128)(2,1)S(1)} %bitcast.176), custom_call_target="tpu_custom_call" | custom-call | bytes 14155776 | tf_op jit(solution)/shard_map/pallas_call | solution.py:222
  256.3 1.7 fusion.66
  258.7 1.8 collective-permute-start.4
  261.2 1.4 collective-permute-done.4
  262.6 1.8 collective-permute-start.5
  266.5 2.8 collective-permute-start.6
  269.3 1.8 collective-permute-done.6
  271.1 2.9 %collective-permute-start.7 = (f32[54,128]{1,0:T(8,128)S(1)}, f32[54,128]{1,0:T(8,128)S(1)}, u32[]{:S(2)}, u32[]{:S(2)}) collective-permute-start(f32[54,128]{1,0:T(8,128)S(1)} %add.173), channel_id=1, source_target_pairs={{0,16},{8,24},{16,0},{24,8},{1,17},{9,25},{17,1},{25,9},{2,18},{10... | collective-permute-start | bytes 82952 | tf_op jit(solution)/shard_map/ppermute | solution.py:259
  (181 shorter events, 38.8 us)
Async XLA Ops:
  0.6 73.6 %copy-start.9 = (bf16[2,128,768]{2,1,0:T(8,128)(2,1)S(1)}, bf16[2,128,768]{2,1,0:T(8,128)(2,1)}, u32[]{:S(2)}) copy-start(bf16[2,128,768]{2,1,0:T(8,128)(2,1)} %param.15) | copy-start | bytes 1179652
  0.7 73.6 %copy-start.43 = (f32[768]{0:T(1024)S(1)}, f32[768]{0:T(1024)}, u32[]{:S(2)}) copy-start(f32[768]{0:T(1024)} %param.18) | copy-start | bytes 9220
  0.7 73.6 %copy-start.29 = (f32[768]{0:T(1024)S(1)}, f32[768]{0:T(1024)}, u32[]{:S(2)}) copy-start(f32[768]{0:T(1024)} %param.17) | copy-start | bytes 9220
  74.2 17.6 %copy-start.2 = (bf16[4,4,48,1536]{3,2,1,0:T(8,128)(2,1)}, bf16[4,4,48,1536]{3,2,1,0:T(8,128)(2,1)S(1)}, u32[]{:S(2)}) copy-start(bf16[4,4,48,1536]{3,2,1,0:T(8,128)(2,1)S(1)} %get-tuple-element.24) | copy-start | bytes 7077892
  94.9 3.4 %copy-start.15 = (bf16[2,512,6,64]{1,3,2,0:T(8,128)(2,1)}, bf16[2,512,6,64]{1,3,2,0:T(8,128)(2,1)S(1)}, u32[]{:S(2)}) copy-start(bf16[2,512,6,64]{1,3,2,0:T(8,128)(2,1)S(1)} %reshape.264) | copy-start | bytes 2359300
  95.1 3.2 %copy-start.22 = (bf16[2,128,6,64]{1,0,3,2:T(2,128)(2,1)}, bf16[2,128,6,64]{1,0,3,2:T(2,128)(2,1)S(1)}, u32[]{:S(2)}) copy-start(bf16[2,128,6,64]{1,0,3,2:T(2,128)(2,1)S(1)} %reshape.263) | copy-start | bytes 589828
  95.2 3.1 %copy-start.25 = (bf16[2,512,6,64]{1,3,2,0:T(8,128)(2,1)S(1)}, bf16[2,512,6,64]{1,3,2,0:T(8,128)(2,1)}, u32[]{:S(2)}) copy-start(bf16[2,512,6,64]{1,3,2,0:T(8,128)(2,1)} %reshape.262) | copy-start | bytes 2359300
  98.3 2.6 copy-start.41
  101.0 2.8 %copy-start.12 = (bf16[2,128,768]{2,1,0:T(8,128)(2,1)S(1)}, bf16[2,128,768]{2,1,0:T(8,128)(2,1)}, u32[]{:S(2)}) copy-start(bf16[2,128,768]{2,1,0:T(8,128)(2,1)} %param.29) | copy-start | bytes 1179652
  101.0 4.1 %copy-start.44 = (f32[768]{0:T(1024)S(1)}, f32[768]{0:T(1024)}, u32[]{:S(2)}) copy-start(f32[768]{0:T(1024)} %param.22) | copy-start | bytes 9220
  101.2 4.1 %copy-start.18 = (bf16[2,128,6,64]{1,0,3,2:T(2,128)(2,1)}, bf16[2,128,6,64]{1,0,3,2:T(2,128)(2,1)S(1)}, u32[]{:S(2)}) copy-start(bf16[2,128,6,64]{1,0,3,2:T(2,128)(2,1)S(1)} %copy.45) | copy-start | bytes 589828
  102.7 2.4 collective-permute-start
  110.1 5.1 %collective-permute-start.2 = (f32[256,768]{1,0:T(8,128)S(1)}, f32[256,768]{1,0:T(8,128)S(1)}, u32[]{:S(2)}, u32[]{:S(2)}) collective-permute-start(f32[256,768]{1,0:T(8,128)S(1)} %fusion.76), channel_id=1, source_target_pairs={{0,1},{1,0},{2,3},{3,2},{4,5},{5,4},{6,7},{7,6},{8,9},{9,8},{10,11... | collective-permute-start | bytes 2359304 | tf_op jit(solution)/shard_map/ppermute | solution.py:247
  111.7 4.5 %collective-permute-start.1 = (f32[256,768]{1,0:T(8,128)S(1)}, f32[256,768]{1,0:T(8,128)S(1)}, u32[]{:S(2)}, u32[]{:S(2)}) collective-permute-start(f32[256,768]{1,0:T(8,128)S(1)} %fusion.65), channel_id=1, source_target_pairs={{0,1},{1,0},{2,3},{3,2},{4,5},{5,4},{6,7},{7,6},{8,9},{9,8},{10,11... | collective-permute-start | bytes 2359304 | tf_op jit(solution)/shard_map/ppermute | solution.py:247
  117.3 5.5 %copy-start.10 = (f32[256,768]{1,0:T(8,128)}, f32[256,768]{1,0:T(8,128)S(1)}, u32[]{:S(2)}) copy-start(f32[256,768]{1,0:T(8,128)S(1)} %get-tuple-element.49) | copy-start | bytes 2359300
  124.4 3.1 %copy-start.17 = (f32[2,6,128,512]{3,2,1,0:T(8,128)S(1)}, f32[2,6,128,512]{3,2,1,0:T(8,128)}, u32[]{:S(2)}) copy-start(f32[2,6,128,512]{3,2,1,0:T(8,128)} %get-tuple-element.73) | copy-start | bytes 9437188
  124.4 3.1 %copy-start.27 = (bf16[2,128,6,64]{1,0,3,2:T(2,128)(2,1)S(1)}, bf16[2,128,6,64]{1,0,3,2:T(2,128)(2,1)}, u32[]{:S(2)}) copy-start(bf16[2,128,6,64]{1,0,3,2:T(2,128)(2,1)} %reshape.269) | copy-start | bytes 589828
  124.4 3.1 %copy-start.42 = (f32[2,6,128]{2,1,0:T(8,128)S(1)}, f32[2,6,128]{2,1,0:T(8,128)}, u32[]{:S(2)}) copy-start(f32[2,6,128]{2,1,0:T(8,128)} %copy-done.41) | copy-start | bytes 18436
  142.8 18.0 %copy-start.24 = (bf16[2,128,6,64]{1,3,2,0:T(8,128)(2,1)S(1)}, bf16[2,128,6,64]{1,3,2,0:T(8,128)(2,1)}, u32[]{:S(2)}) copy-start(bf16[2,128,6,64]{1,3,2,0:T(8,128)(2,1)} %get-tuple-element.77) | copy-start | bytes 589828
  161.2 3.4 %copy-start.26 = (bf16[256,384]{1,0:T(8,128)(2,1)}, bf16[256,384]{1,0:T(8,128)(2,1)S(1)}, u32[]{:S(2)}) copy-start(bf16[256,384]{1,0:T(8,128)(2,1)S(1)} %copy.53) | copy-start | bytes 589828
  161.2 3.4 %copy-start.39 = (f32[384]{0:T(512)S(1)}, f32[384]{0:T(512)}, u32[]{:S(2)}) copy-start(f32[384]{0:T(512)} %get-tuple-element.45) | copy-start | bytes 4612
  161.3 4.8 %copy-start.21 = (bf16[256,768]{1,0:T(8,128)(2,1)S(1)}, bf16[256,768]{1,0:T(8,128)(2,1)}, u32[]{:S(2)}) copy-start(bf16[256,768]{1,0:T(8,128)(2,1)} %copy-done.20) | copy-start | bytes 1179652
  161.3 5.7 %copy-start.19 = (bf16[2,128,6,64]{1,0,3,2:T(2,128)(2,1)S(1)}, bf16[2,128,6,64]{1,0,3,2:T(2,128)(2,1)}, u32[]{:S(2)}) copy-start(bf16[2,128,6,64]{1,0,3,2:T(2,128)(2,1)} %copy-done.18) | copy-start | bytes 589828
  164.6 91.7 %collective-permute-start.3 = (f32[256,768]{1,0:T(8,128)}, f32[256,768]{1,0:T(8,128)}, u32[]{:S(2)}, u32[]{:S(2)}) collective-permute-start(f32[256,768]{1,0:T(8,128)} %fusion.12), channel_id=1, source_target_pairs={{0,1},{1,0},{2,3},{3,2},{4,5},{5,4},{6,7},{7,6},{8,9},{9,8},{10,11... | collective-permute-start | bytes 2359304 | tf_op jit(solution)/shard_map/ppermute | solution.py:247
  256.3 2.4 copy-start.40
  258.0 16.0 %copy-start.11 = (f32[256,768]{1,0:T(8,128)S(1)}, f32[256,768]{1,0:T(8,128)}, u32[]{:S(2)}) copy-start(f32[256,768]{1,0:T(8,128)} %copy-done.10) | copy-start | bytes 2359300
  258.0 16.0 %copy-start.14 = (bf16[2,128,768]{2,1,0:T(8,128)(2,1)S(1)}, bf16[2,128,768]{2,1,0:T(8,128)(2,1)}, u32[]{:S(2)}) copy-start(bf16[2,128,768]{2,1,0:T(8,128)(2,1)} %param.29) | copy-start | bytes 1179652
  258.0 16.0 %copy-start.38 = (f32[256]{0:T(256)S(1)}, f32[256]{0:T(256)}, u32[]{:S(2)}) copy-start(f32[256]{0:T(256)} %copy-done.37) | copy-start | bytes 3076
  258.7 3.9 %collective-permute-start.4 = (f32[54,128]{1,0:T(8,128)S(1)}, f32[54,128]{1,0:T(8,128)S(1)}, u32[]{:S(2)}, u32[]{:S(2)}) collective-permute-start(f32[54,128]{1,0:T(8,128)S(1)} %bitcast.208), channel_id=1, source_target_pairs={{0,2},{2,0},{4,6},{6,4},{1,3},{3,1},{5,7},{7,5},{8,10},{10,8},{12,... | collective-permute-start | bytes 82952 | tf_op jit(solution)/shard_map/ppermute | solution.py:259
  262.6 3.9 %collective-permute-start.5 = (f32[54,128]{1,0:T(8,128)S(1)}, f32[54,128]{1,0:T(8,128)S(1)}, u32[]{:S(2)}, u32[]{:S(2)}) collective-permute-start(f32[54,128]{1,0:T(8,128)S(1)} %bitcast_add_fusion.1), channel_id=1, source_target_pairs={{0,4},{2,6},{4,0},{6,2},{1,5},{3,7},{5,1},{7,3},{8,12},{10,14},{12... | collective-permute-start | bytes 82952 | tf_op jit(solution)/shard_map/ppermute | solution.py:259
  266.5 4.6 %collective-permute-start.6 = (f32[54,128]{1,0:T(8,128)S(1)}, f32[54,128]{1,0:T(8,128)S(1)}, u32[]{:S(2)}, u32[]{:S(2)}) collective-permute-start(f32[54,128]{1,0:T(8,128)S(1)} %fusion.96), channel_id=1, source_target_pairs={{0,8},{8,0},{16,24},{24,16},{1,9},{9,1},{17,25},{25,17},{2,10},{10... | collective-permute-start | bytes 82952 | tf_op jit(solution)/shard_map/ppermute | solution.py:259
  271.1 4.8 %collective-permute-start.7 = (f32[54,128]{1,0:T(8,128)S(1)}, f32[54,128]{1,0:T(8,128)S(1)}, u32[]{:S(2)}, u32[]{:S(2)}) collective-permute-start(f32[54,128]{1,0:T(8,128)S(1)} %add.173), channel_id=1, source_target_pairs={{0,16},{8,24},{16,0},{24,8},{1,17},{9,25},{17,1},{25,9},{2,18},{10... | collective-permute-start | bytes 82952 | tf_op jit(solution)/shard_map/ppermute | solution.py:259
  (26 other events, 38.8 us)

commit v2 on v1

--- a/solution.py
+++ b/solution.py
@@ -10,6 +10,7 @@
 
 HEAD = 64
 MESH = pl.DeviceIdType.MESH
+AHEAD = 3
 
 
 def partners(z_peers):
@@ -134,8 +135,16 @@
 
 
 def scatter_kernel(arrays, slots, z_peers, *refs):
-    ins, outs = refs[:arrays], refs[arrays : 2 * arrays]
-    per = refs[2 * arrays :]
+    ins = refs[:arrays]
+    refs = refs[arrays:]
+    if z_peers:
+        small_in, refs = refs[0], refs[1:]
+    outs = refs[:arrays]
+    refs = refs[arrays:]
+    if z_peers:
+        small_out, pair, pair_in, small_all, p_send, p_recv, s_send, s_recv = (refs[0],) + tuple(refs[-7:])
+        refs = refs[1:-7]
+    per = refs
     first, mixed, second = per[:arrays], per[arrays : 2 * arrays], per[2 * arrays : 3 * arrays]
     rest = per[3 * arrays :]
     if z_peers:
@@ -160,7 +169,31 @@
     def ways(k, s):
         return (side, over) if (k + s) % 2 == 0 else (over, side)
 
-    for k, s in order:
+    def small_pair(stage):
+        src = small_in if stage == 0 else pair
+        go(remote(src, pair_in.at[stage], p_send.at[stage], p_recv.at[stage], "ctx", (side, over)[stage]))
+
+    def small_add(stage):
+        ref = pair_in.at[stage]
+        remote(ref, ref, p_send.at[stage], p_recv.at[stage], "ctx", side).wait_recv()
+        if stage == 0:
+            pair[...] = small_in[...] + ref[...]
+            small_pair(1)
+        else:
+            small_all[me_f] = pair[...] + ref[...]
+            for t in range(1, slots):
+                go(remote(small_all.at[me_f], small_all.at[me_f], s_send.at[t], s_recv.at[slots - t], "fsdp", peers[t - 1]))
+
+    def small_end():
+        for s in range(1, slots):
+            ref = small_all.at[slot(s)]
+            remote(ref, ref, s_send.at[s], s_recv.at[s], "fsdp", peers[0]).wait_recv()
+        total = small_all[0]
+        for s in range(1, slots):
+            total = total + small_all[s]
+        small_out[...] = total
+
+    def first_send(k, s):
         near, other = ways(k, s)
         go(remote(ins[k].at[slot(s), across], first[k].at[s, 1], a_send.at[1, k, s], a_recv.at[1, k, s], "ctx", near))
         go(remote(ins[k].at[slot(s), near], first[k].at[s, 0], a_send.at[0, k, s], a_recv.at[0, k, s], "ctx", near))
@@ -187,9 +220,18 @@
             z_out[k][s] = total.astype(jnp.bfloat16)
             go(remote(z_out[k].at[s], z_in[k].at[slots - s], z_send.at[k, s], z_recv.at[k, slots - s], "fsdp", peers[s - 1]))
 
-    lag = 3 if len(order) > 4 else len(order)
+    lag = 2 if z_peers else len(order)
+    ahead = min(AHEAD, len(order))
+    if z_peers:
+        small_pair(0)
+    for k, s in order[:ahead]:
+        first_send(k, s)
     for at, (k, s) in enumerate(order):
         middle(k, s)
+        if at + ahead < len(order):
+            first_send(*order[at + ahead])
+        if z_peers and at in (0, 1):
+            small_add(at)
         if at >= lag:
             last(*order[at - lag])
     for k, s in order[len(order) - lag :]:
@@ -202,11 +244,12 @@
                 remote(ref, ref, z_send.at[k, s], z_recv.at[k, s], "fsdp", peers[0]).wait_recv()
                 total = total + ref[...].astype(f32)
             outs[k][0] = total
+        small_end()
     for copy in started:
         copy.wait_send()
 
 
-def scatter_blocks(parts, z_peers, collective_id):
+def scatter_blocks(parts, z_peers, collective_id, small=None):
     arrays = len(parts)
     slots = parts[0].shape[0]
     bf16 = jnp.bfloat16
@@ -218,18 +261,26 @@
         scratch += [pltpu.VMEM((slots,) + d, bf16) for d in dims] * 2
     scratch += [pltpu.SemaphoreType.DMA((2, arrays, slots))] * 2
     scratch += [pltpu.SemaphoreType.DMA((arrays, slots))] * 4
+    out_shape = [jax.ShapeDtypeStruct((1 if z_peers else slots,) + d, jnp.float32) for d in dims]
+    extra = []
+    if z_peers:
+        extra = [small]
+        out_shape.append(jax.ShapeDtypeStruct(small.shape, small.dtype))
+        scratch += [pltpu.VMEM(small.shape, small.dtype), pltpu.VMEM((2,) + small.shape, small.dtype)]
+        scratch += [pltpu.VMEM((slots,) + small.shape, small.dtype)]
+        scratch += [pltpu.SemaphoreType.DMA((2,))] * 2 + [pltpu.SemaphoreType.DMA((slots,))] * 2
     size = sum(x.size * 2 for x in parts)
     return pl.pallas_call(
         functools.partial(scatter_kernel, arrays, slots, z_peers),
-        out_shape=[jax.ShapeDtypeStruct((1 if z_peers else slots,) + d, jnp.float32) for d in dims],
-        in_specs=[spec] * arrays,
-        out_specs=[spec] * arrays,
+        out_shape=out_shape,
+        in_specs=[spec] * (arrays + len(extra)),
+        out_specs=[spec] * len(out_shape),
         scratch_shapes=scratch,
         compiler_params=pltpu.CompilerParams(
             collective_id=collective_id, has_side_effects=True, vmem_limit_bytes=int(size * 3) + (6 << 20)
         ),
         cost_estimate=pl.CostEstimate(flops=0, bytes_accessed=2 * size, transcendentals=0),
-    )(*parts)
+    )(*parts, *extra)
 
 
 def norm_rows(rows_in, row_gain, row_shift):
@@ -249,20 +300,16 @@
     return total
 
 
-def sum_small(arrays):
-    sizes = [x.size for x in arrays]
-    packed = jnp.concatenate([x.reshape(-1) for x in arrays]).reshape(-1, 128)
-    for axis in ("ctx", "fsdp"):
-        count = lax.axis_size(axis)
-        bit = 1
-        while bit < count:
-            packed = packed + lax.ppermute(packed, axis, [(i, i ^ bit) for i in range(count)])
-            bit *= 2
+def pack_small(arrays):
+    return jnp.pad(jnp.concatenate([x.reshape(-1) for x in arrays]).reshape(-1, 128), ((0, -sum(x.size for x in arrays) // 128 % 8), (0, 0)))
+
+
+def unpack_small(packed, arrays):
     flat = packed.reshape(-1)
     result, at = [], 0
-    for x, size in zip(arrays, sizes):
-        result.append(flat[at : at + size].reshape(x.shape))
-        at += size
+    for x in arrays:
+        result.append(flat[at : at + x.size].reshape(x.shape))
+        at += x.size
     return result
 
 
@@ -273,12 +320,14 @@
     return [lax.all_gather(x, ("fsdp", "ctx"), axis=0, tiled=True) for x in shards]
 
 
-def scatter_weights(parts):
+def scatter_weights(parts, small):
     slots = lax.axis_size("fsdp")
     if slots <= 4:
         blocks = [x.astype(jnp.bfloat16).reshape(slots, 4, -1, x.shape[-1]) for x in parts]
-        return [x[0] for x in scatter_blocks(blocks, True, 2)]
-    return [lax.psum_scatter(x, ("fsdp", "ctx"), scatter_dimension=0, tiled=True) for x in parts]
+        *sums, total = scatter_blocks(blocks, True, 2, small)
+        return [x[0] for x in sums], total
+    sums = [lax.psum_scatter(x, ("fsdp", "ctx"), scatter_dimension=0, tiled=True) for x in parts]
+    return sums, lax.psum(small, ("fsdp", "ctx"))
 
 
 def body(
@@ -405,25 +454,24 @@
     first_back = jax.vjp(norm_rows, inputs, first_gain, first_shift)[1]
     grad_in_norm, grad_firstgain, grad_firstshift = first_back(grad_normed)
     grad_input = (grad_residual + grad_in_norm).reshape(seq_count, span, width)
-    first_sum, up_sum, down_sum = scatter_weights([grad_first, grad_upweight, grad_downweight])
+    small_parts = (
+        grad_firstgain,
+        grad_firstshift,
+        grad_qvbias,
+        grad_outbias,
+        grad_secondgain,
+        grad_secondshift,
+        grad_upbias,
+        grad_downbias,
+    )
+    (first_sum, up_sum, down_sum), small_total = scatter_weights([grad_first, grad_upweight, grad_downweight], pack_small(small_parts))
     weight_grads = (
         jnp.stack([first_sum[:, k * local_width : (k + 1) * local_width] for k in range(3)]),
         first_sum[:, 3 * local_width :].T,
         up_sum,
         down_sum.T,
     )
-    small_sums = sum_small(
-        (
-            grad_firstgain,
-            grad_firstshift,
-            grad_qvbias,
-            grad_outbias,
-            grad_secondgain,
-            grad_secondshift,
-            grad_upbias,
-            grad_downbias,
-        )
-    )
+    small_sums = unpack_small(small_total, small_parts)
     return (
         layer_output,
         grad_input,

time: 280 us -> 253 us (0.904)
  Pallas kernels: 182 us -> 171 us
  starting transfers between devices: 9.99 us -> 0.71 us
  waiting for transfers between devices: 6.5 us -> 1.2 us
    pallas_call x2, Pallas kernels: 100 us -> 89.9 us  [scatter_blocks(): pl.pallas_call(functools.partial(scatter_kernel, arrays, slots, z_peers),...]
    ppermute x4 -> x0, starting transfers between devices: 9.27 us -> none  [sum_small(): lax.ppermute(packed, axis, [(i, i ^ bit) for i in range(count)])]
    ppermute x4 -> x0, waiting for transfers between devices: 5.28 us -> none  [sum_small(): lax.ppermute(packed, axis, [(i, i ^ bit) for i in range(count)])]
    unnamed x110 -> x104, local copies, waits for them, and re-layouts: 10.6 us -> 11.1 us
  transfers between devices with their start and end apart: 8 -> 4, of which waited for: 5 -> 1; matrix products, arithmetic and copies ran while one was open for 5% -> 5% of each run, Pallas kernels for 30% -> 0%
where the time goes in v2:
time: 253 us; the launch traced here: 252 us
  Pallas kernels  171 us (68%)
  local copies, waits for them, and re-layouts  32.1 us (13%)
  matrix products  31.4 us (12%)
  other arithmetic  14.5 us (6%)
    pallas_call x2, Pallas kernels, scatter_blocks(): pl.pallas_call(functools.partial(scatter_kernel, arrays, slots, z_peers),...  89.9 us
    pallas_call x2, Pallas kernels, gather_blocks(): pl.pallas_call(functools.partial(gather_kernel, arrays, slots, z_peers),...  81.3 us
    unnamed x104, local copies, waits for them, and re-layouts  11.1 us
    reshape x4, local copies, waits for them, and re-layouts, body(): x.astype(bf16).reshape(seq_count, 4, span, local_width)  7.24 us
  transfers between devices with their start and end apart: 4, of which 1 were waited for; matrix products, arithmetic and copies ran while one was open for 5% of the time, Pallas kernels for 0%

profile of v2, /device:TPU:0, one launch (start us, length us, event | category | flops | bytes accessed | tf_op | source)
XLA Modules:
  0.0 252.4 jit_solution(15483163936817703813)
XLA Ops:
  1.5 1.1 convert_reduce_fusion.1
  2.7 1.2 fusion.31
  6.6 64.8 %shard_map.254 = (bf16[4,4,48,1536]{3,2,1,0:T(8,128)(2,1)S(1)}, bf16[4,4,48,1536]{3,2,1,0:T(8,128)(2,1)S(1)}, bf16[4,4,48,1536]{3,2,1,0:T(8,128)(2,1)S(1)}) custom-call(bf16[1,48,1536]{2,1,0:T(8,128)(2,1)S(1)} %maximum_bitcast_fusion.refs_0_, bf16[1,48,1536]{2,1,0:T(8,128)(2,1)S(1)} %bitcast.183, bf16[1,48,1536]{2,1,0:T(8,128)(2,1)S(1)} %bitcast.184), custom_call_target="tpu_custom_call" | custom-call | bytes 14155776 | tf_op jit(solution)/shard_map/pallas_call | solution.py:119
  71.4 1.4 copy-done.5
  72.8 1.5 copy-done.7
  75.8 16.5 %shard_map.255 = (bf16[2,4,128,384]{3,2,1,0:T(8,128)(2,1)S(1)}, bf16[2,4,128,384]{3,2,1,0:T(8,128)(2,1)S(1)}) custom-call(bf16[2,128,384]{2,1,0:T(8,128)(2,1)S(1)} %bitcast.175, bf16[2,128,384]{2,1,0:T(8,128)(2,1)S(1)} %bitcast.174), custom_call_target="tpu_custom_call" | custom-call | bytes 3145728 | tf_op jit(solution)/shard_map/pallas_call | solution.py:119
  92.9 1.2 reshape.262
  95.7 3.1 %fusion.71 = (f32[2,6,128]{2,1,0:T(8,128)S(1)}, f32[2,6,128,512]{3,2,1,0:T(8,128)}) fusion(pred[2,128,512]{2,1,0:T(8,128)(4,1)S(1)} %broadcast_and_fusion, bf16[2,512,6,64]{1,3,2,0:T(8,128)(2,1)S(1)} %reshape.264, bf16[2,128,6,64]{1,0,3,2:T(2,128)(2,1)S(1)} %reshape.263), kind=kOutput, calls=%fused_computation.149 | convolution fusion | flops 104595968 | bytes 4265984 | tf_op jit(solution)/shard_map/sub | solution.py:388
  98.8 2.6 %fusion.19 = bf16[2,128,6,64]{1,3,2,0:T(8,128)(2,1)S(1)} fusion(bf16[2,512,6,64]{1,3,2,0:T(8,128)(2,1)S(1)} %copy-done.25, f32[2,6,128,512]{3,2,1,0:T(8,128)} %get-tuple-element.75, f32[2,6,128]{2,1,0:T(8,128)S(1)} %get-tuple-element.74), kind=kOutput, calls=%fused_computation.42 | convolution fusion | flops 102334464 | bytes 4134912 | tf_op jit(solution)/shard_map/shun,snhe->suhe/dot_general | solution.py:393
  102.3 1.5 fusion.37
  105.0 1.2 collective-permute-done
  108.3 2.0 convert_reduce_fusion
  112.9 2.4 convolution_convert_fusion
  117.2 1.1 fusion.68
  120.0 2.1 convolution_convert_fusion.6
  122.1 1.7 copy.46
  123.8 1.7 reshape.269
  125.5 3.1 %multiply_reduce_fusion = (f32[2,6,128]{2,1,0:T(8,128)S(1)}, f32[2,6,128,512]{3,2,1,0:T(8,128)S(1)}) fusion(f32[2,6,128,512]{3,2,1,0:T(8,128)} %get-tuple-element.75, f32[2,6,128]{2,1,0:T(8,128)} %copy-done.38, bf16[2,512,6,64]{1,3,2,0:T(8,128)(2,1)} %reshape.262, bf16[2,128,6,64]{1,0,3,2:T(2,128)(2,1)} %reshape.269), kind=kOutput, calls=%fused_computation.5 | convolution fusion | flops 103021056 | bytes 7286784 | tf_op jit(solution)/shard_map/suhe,snhe->shun/dot_general | solution.py:424
  128.6 1.4 fusion.17
  132.1 1.9 convert_reduce_fusion.5
  135.1 1.5 copy.51.refs_0_
  136.6 2.4 reshape.272
  139.1 2.2 copy.52.refs_1_
  141.3 1.1 copy-done
  142.4 16.0 %shard_map.256 = (f32[2,128,384]{2,1,0:T(8,128)S(1)}, f32[2,128,384]{2,1,0:T(8,128)S(1)}) custom-call(bf16[2,4,128,384]{3,2,1,0:T(8,128)(2,1)S(1)} %copy.51.refs_0_, bf16[2,4,128,384]{3,2,1,0:T(8,128)(2,1)S(1)} %copy-done), custom_call_target="tpu_custom_call" | custom-call | bytes 3145728 | tf_op jit(solution)/shard_map/pallas_call | solution.py:273
  158.5 1.3 convert_reduce_fusion.4
  160.9 3.3 %fusion.12 = f32[256,768]{1,0:T(8,128)} fusion(bf16[768,1536]{1,0:T(8,128)(2,1)} %bitcast.182, bf16[256,384]{1,0:T(8,128)(2,1)} %bitcast.201, bf16[256,384]{1,0:T(8,128)(2,1)} %bitcast.203, bf16[256,384]{1,0:T(8,128)(2,1)S(1)} %copy.53), kind=kOutput, calls=%fused_computation.28 | convolution fusion | flops 454754304 | bytes 3145728 | tf_op jit(solution)/shard_map/rc,dc->rd/dot_general | solution.py:453
  166.6 1.4 convolution_convert_fusion.4
  168.0 1.8 convolution_convert_fusion.2
  170.2 1.8 fusion.66
  172.7 73.8 %shard_map.257 = (f32[1,48,1536]{2,1,0:T(8,128)S(1)}, f32[1,48,1536]{2,1,0:T(8,128)S(1)}, f32[1,48,1536]{2,1,0:T(8,128)S(1)}, f32[56,128]{1,0:T(8,128)S(1)}) custom-call(bf16[4,4,48,1536]{3,2,1,0:T(8,128)(2,1)S(1)} %pad_maximum_fusion.refs_0_, bf16[4,4,48,1536]{3,2,1,0:T(8,128)(2,1)S(1)} %bitcast.172, bf16[4,4,48,1536]{3,2,1,0:T(8,128)(2,1)S(1)} %bitcast.173, ...), custom_call_target="tpu_custom_call" | custom-call | bytes 14155776 | tf_op jit(solution)/shard_map/pallas_call | solution.py:273
  247.7 1.3 add_add_fusion.2
  (164 shorter events, 29.4 us)
Async XLA Ops:
  0.6 73.6 %copy-start.9 = (bf16[2,128,768]{2,1,0:T(8,128)(2,1)S(1)}, bf16[2,128,768]{2,1,0:T(8,128)(2,1)}, u32[]{:S(2)}) copy-start(bf16[2,128,768]{2,1,0:T(8,128)(2,1)} %param.15) | copy-start | bytes 1179652
  0.7 73.6 %copy-start.40 = (f32[768]{0:T(1024)S(1)}, f32[768]{0:T(1024)}, u32[]{:S(2)}) copy-start(f32[768]{0:T(1024)} %param.18) | copy-start | bytes 9220
  0.7 73.6 %copy-start.27 = (f32[768]{0:T(1024)S(1)}, f32[768]{0:T(1024)}, u32[]{:S(2)}) copy-start(f32[768]{0:T(1024)} %param.17) | copy-start | bytes 9220
  92.3 1.8 copy-start.45
  95.4 3.4 %copy-start.15 = (bf16[2,512,6,64]{1,3,2,0:T(8,128)(2,1)}, bf16[2,512,6,64]{1,3,2,0:T(8,128)(2,1)S(1)}, u32[]{:S(2)}) copy-start(bf16[2,512,6,64]{1,3,2,0:T(8,128)(2,1)S(1)} %reshape.264) | copy-start | bytes 2359300
  95.6 3.2 %copy-start.22 = (bf16[2,128,6,64]{1,0,3,2:T(2,128)(2,1)}, bf16[2,128,6,64]{1,0,3,2:T(2,128)(2,1)S(1)}, u32[]{:S(2)}) copy-start(bf16[2,128,6,64]{1,0,3,2:T(2,128)(2,1)S(1)} %reshape.263) | copy-start | bytes 589828
  95.7 3.1 %copy-start.25 = (bf16[2,512,6,64]{1,3,2,0:T(8,128)(2,1)S(1)}, bf16[2,512,6,64]{1,3,2,0:T(8,128)(2,1)}, u32[]{:S(2)}) copy-start(bf16[2,512,6,64]{1,3,2,0:T(8,128)(2,1)} %reshape.262) | copy-start | bytes 2359300
  98.8 2.6 %copy-start.38 = (f32[2,6,128]{2,1,0:T(8,128)}, f32[2,6,128]{2,1,0:T(8,128)S(1)}, u32[]{:S(2)}) copy-start(f32[2,6,128]{2,1,0:T(8,128)S(1)} %get-tuple-element.74) | copy-start | bytes 18436
  101.4 3.4 %copy-start.12 = (bf16[2,128,768]{2,1,0:T(8,128)(2,1)S(1)}, bf16[2,128,768]{2,1,0:T(8,128)(2,1)}, u32[]{:S(2)}) copy-start(bf16[2,128,768]{2,1,0:T(8,128)(2,1)} %param.29) | copy-start | bytes 1179652
  101.4 4.7 %copy-start.41 = (f32[768]{0:T(1024)S(1)}, f32[768]{0:T(1024)}, u32[]{:S(2)}) copy-start(f32[768]{0:T(1024)} %param.22) | copy-start | bytes 9220
  103.8 2.4 collective-permute-start
  104.9 1.7 copy-start.28
  111.2 5.1 %collective-permute-start.2 = (f32[256,768]{1,0:T(8,128)S(1)}, f32[256,768]{1,0:T(8,128)S(1)}, u32[]{:S(2)}, u32[]{:S(2)}) collective-permute-start(f32[256,768]{1,0:T(8,128)S(1)} %fusion.76), channel_id=1, source_target_pairs={{0,1},{1,0},{2,3},{3,2},{4,5},{5,4},{6,7},{7,6},{8,9},{9,8},{10,11... | collective-permute-start | bytes 2359304 | tf_op jit(solution)/shard_map/ppermute | solution.py:298
  112.7 4.5 %collective-permute-start.1 = (f32[256,768]{1,0:T(8,128)S(1)}, f32[256,768]{1,0:T(8,128)S(1)}, u32[]{:S(2)}, u32[]{:S(2)}) collective-permute-start(f32[256,768]{1,0:T(8,128)S(1)} %fusion.65), channel_id=1, source_target_pairs={{0,1},{1,0},{2,3},{3,2},{4,5},{5,4},{6,7},{7,6},{8,9},{9,8},{10,11... | collective-permute-start | bytes 2359304 | tf_op jit(solution)/shard_map/ppermute | solution.py:298
  118.3 5.5 %copy-start.10 = (f32[256,768]{1,0:T(8,128)}, f32[256,768]{1,0:T(8,128)S(1)}, u32[]{:S(2)}) copy-start(f32[256,768]{1,0:T(8,128)S(1)} %get-tuple-element.51) | copy-start | bytes 2359300
  125.5 3.1 %copy-start.17 = (f32[2,6,128,512]{3,2,1,0:T(8,128)S(1)}, f32[2,6,128,512]{3,2,1,0:T(8,128)}, u32[]{:S(2)}) copy-start(f32[2,6,128,512]{3,2,1,0:T(8,128)} %get-tuple-element.75) | copy-start | bytes 9437188
  125.5 3.1 %copy-start.26 = (bf16[2,128,6,64]{1,0,3,2:T(2,128)(2,1)S(1)}, bf16[2,128,6,64]{1,0,3,2:T(2,128)(2,1)}, u32[]{:S(2)}) copy-start(bf16[2,128,6,64]{1,0,3,2:T(2,128)(2,1)} %reshape.269) | copy-start | bytes 589828
  125.5 3.1 %copy-start.39 = (f32[2,6,128]{2,1,0:T(8,128)S(1)}, f32[2,6,128]{2,1,0:T(8,128)}, u32[]{:S(2)}) copy-start(f32[2,6,128]{2,1,0:T(8,128)} %copy-done.38) | copy-start | bytes 18436
  142.4 18.0 %copy-start.24 = (bf16[2,128,6,64]{1,3,2,0:T(8,128)(2,1)S(1)}, bf16[2,128,6,64]{1,3,2,0:T(8,128)(2,1)}, u32[]{:S(2)}) copy-start(bf16[2,128,6,64]{1,3,2,0:T(8,128)(2,1)} %get-tuple-element.79) | copy-start | bytes 589828
  160.9 3.4 %copy-start.21 = (bf16[256,768]{1,0:T(8,128)(2,1)S(1)}, bf16[256,768]{1,0:T(8,128)(2,1)}, u32[]{:S(2)}) copy-start(bf16[256,768]{1,0:T(8,128)(2,1)} %copy-done.20) | copy-start | bytes 1179652
  160.9 5.8 %copy-start.19 = (bf16[2,128,6,64]{1,0,3,2:T(2,128)(2,1)S(1)}, bf16[2,128,6,64]{1,0,3,2:T(2,128)(2,1)}, u32[]{:S(2)}) copy-start(bf16[2,128,6,64]{1,0,3,2:T(2,128)(2,1)} %copy-done.18) | copy-start | bytes 589828
  164.2 6.0 %collective-permute-start.3 = (f32[256,768]{1,0:T(8,128)}, f32[256,768]{1,0:T(8,128)}, u32[]{:S(2)}, u32[]{:S(2)}) collective-permute-start(f32[256,768]{1,0:T(8,128)} %fusion.12), channel_id=1, source_target_pairs={{0,1},{1,0},{2,3},{3,2},{4,5},{5,4},{6,7},{7,6},{8,9},{9,8},{10,11... | collective-permute-start | bytes 2359304 | tf_op jit(solution)/shard_map/ppermute | solution.py:298
  170.1 1.9 copy-start.34
  170.1 2.4 copy-start.29
  170.1 2.4 copy-start.32
  170.1 2.4 copy-start.31
  170.2 2.4 copy-start.30
  170.2 2.4 copy-start.37
  170.2 2.5 copy-start.1
  172.7 75.1 %copy-start.11 = (f32[256,768]{1,0:T(8,128)S(1)}, f32[256,768]{1,0:T(8,128)}, u32[]{:S(2)}) copy-start(f32[256,768]{1,0:T(8,128)} %copy-done.10) | copy-start | bytes 2359300
  172.7 75.1 %copy-start.14 = (bf16[2,128,768]{2,1,0:T(8,128)(2,1)S(1)}, bf16[2,128,768]{2,1,0:T(8,128)(2,1)}, u32[]{:S(2)}) copy-start(bf16[2,128,768]{2,1,0:T(8,128)(2,1)} %param.29) | copy-start | bytes 1179652
  172.7 75.1 %copy-start.36 = (f32[256]{0:T(256)S(1)}, f32[256]{0:T(256)}, u32[]{:S(2)}) copy-start(f32[256]{0:T(256)} %copy-done.35) | copy-start | bytes 3076
  (19 other events, 22.5 us)

commit v3 on v2

--- a/solution.py
+++ b/solution.py
@@ -328,6 +328,55 @@
         return [x[0] for x in sums], total
     sums = [lax.psum_scatter(x, ("fsdp", "ctx"), scatter_dimension=0, tiled=True) for x in parts]
     return sums, lax.psum(small, ("fsdp", "ctx"))
+
+
+def product(left, right, left_dim, right_dim):
+    return lax.dot_general(
+        left, right, (((left_dim,), (right_dim,)), ((), ())), preferred_element_type=jnp.float32
+    )
+
+
+def attend_kernel(scale, lengths, q_ref, k_ref, v_ref, probs_ref, out_ref):
+    seqs, heads, span, total = probs_ref.shape
+    rows = lax.axis_index("ctx") * span + lax.broadcasted_iota(jnp.int32, (span, total), 0)
+    keys = lax.broadcasted_iota(jnp.int32, (span, total), 1)
+    for s in range(seqs):
+        allowed = (keys <= rows) & (keys < lengths[s])
+        for h in range(heads):
+            at, cols = slice(s * span, (s + 1) * span), slice(h * HEAD, (h + 1) * HEAD)
+            scores = product(q_ref[at, cols], k_ref[s, :, cols], 1, 1) * scale
+            masked = jnp.where(allowed, scores, -1e30)
+            peak = jnp.max(masked, axis=-1, keepdims=True)
+            expo = jnp.where(allowed, jnp.exp(masked - peak), 0.0)
+            probs = expo / jnp.sum(expo, axis=-1, keepdims=True)
+            probs_ref[s, h] = probs
+            out_ref[at, cols] = product(probs.astype(jnp.bfloat16), v_ref[s, :, cols], 1, 0).astype(jnp.bfloat16)
+
+
+def attend_back_kernel(scale, q_ref, k_ref, v_ref, probs_ref, grad_ref, gq_ref, gk_ref, gv_ref):
+    seqs, heads, span, _ = probs_ref.shape
+    bf16 = jnp.bfloat16
+    for s in range(seqs):
+        for h in range(heads):
+            at, cols = slice(s * span, (s + 1) * span), slice(h * HEAD, (h + 1) * HEAD)
+            probs, grad, keys = probs_ref[s, h], grad_ref[at, cols], k_ref[s, :, cols]
+            grad_probs = product(grad, v_ref[s, :, cols], 1, 1)
+            inner = jnp.sum(probs * grad_probs, axis=-1, keepdims=True)
+            grad_scores = (probs * (grad_probs - inner)).astype(bf16)
+            gq_ref[at, cols] = (product(grad_scores, keys, 1, 0) * scale).astype(bf16)
+            gk_ref[s, :, cols] = (product(grad_scores, q_ref[at, cols], 0, 0) * scale).astype(bf16)
+            gv_ref[s, :, cols] = product(probs.astype(bf16), grad, 0, 0).astype(bf16)
+
+
+def local_call(kernel, outs, args, scalars=0):
+    spec = pl.BlockSpec(memory_space=pltpu.VMEM)
+    return pl.pallas_call(
+        kernel,
+        out_shape=[jax.ShapeDtypeStruct(dims, kind) for dims, kind in outs],
+        in_specs=[pl.BlockSpec(memory_space=pltpu.SMEM)] * scalars + [spec] * (len(args) - scalars),
+        out_specs=[spec] * len(outs),
+        compiler_params=pltpu.CompilerParams(vmem_limit_bytes=24 << 20),
+    )(*args)
 
 
 def body(
@@ -368,30 +417,13 @@
     key_all, value_all = gather_blocks(
         [x.reshape(seq_count, span, local_width) for x in (key_local, value_local)], seq_count, False, 3
     )
-    query_heads = queries.reshape(seq_count, span, head_count, HEAD)
-    query_pos = lax.axis_index("ctx") * span + jnp.arange(span, dtype=jnp.int32)
-    key_pos = jnp.arange(full_length, dtype=jnp.int32)
-    allowed = (key_pos[None, :] <= query_pos[:, None])[None, None] & (
-        key_pos[None, None, None, :] < lengths[:, None, None, None]
-    )
-
-    def masked_scores(key_source):
-        key_heads = key_source.reshape(seq_count, full_length, head_count, HEAD)
-        scores = (
-            jnp.einsum("suhe,snhe->shun", query_heads, key_heads, preferred_element_type=f32)
-            * score_scale
-        )
-        return jnp.where(allowed, scores, -1e30)
-
-    masked = masked_scores(key_all)
-    peak = jnp.max(masked, axis=-1, keepdims=True)
-    expo = jnp.where(allowed, jnp.exp(masked - peak), 0.0)
-    row_total = jnp.sum(expo, axis=-1, keepdims=True)
-    probs = expo / row_total
-    probs_low = probs.astype(bf16)
-    value_heads = value_all.reshape(seq_count, full_length, head_count, HEAD)
-    attended = jnp.einsum("shun,snhe->suhe", probs_low, value_heads, preferred_element_type=f32)
-    attended = attended.reshape(row_count, local_width).astype(bf16)
+    key_all, value_all = (x.reshape(seq_count, full_length, local_width) for x in (key_all, value_all))
+    probs, attended = local_call(
+        functools.partial(attend_kernel, score_scale),
+        [((seq_count, head_count, span, full_length), f32), ((row_count, local_width), bf16)],
+        [lengths, queries, key_all, value_all],
+        1,
+    )
     residual = inputs + head_sum(jnp.einsum("rc,dc->rd", attended, out_full, preferred_element_type=f32)) + out_bias
     normed_two_low = norm_rows(residual, second_gain, second_shift).astype(bf16)
     up_proj = jnp.dot(normed_two_low, up_full, preferred_element_type=f32) + up_bias
@@ -416,30 +448,14 @@
     grad_attended = jnp.einsum(
         "rd,dc->rc", grad_branch, out_full, preferred_element_type=f32
     ).astype(bf16)
-    probs_again = probs
-    probs_low_again = probs_low
-    key_heads_back = key_all.reshape(seq_count, full_length, head_count, HEAD)
-    value_heads_back = value_all.reshape(seq_count, full_length, head_count, HEAD)
-    grad_att_heads = grad_attended.reshape(seq_count, span, head_count, HEAD)
-    grad_probs = jnp.einsum(
-        "suhe,snhe->shun", grad_att_heads, value_heads_back, preferred_element_type=f32
-    )
-    inner_total = jnp.sum(probs_again * grad_probs, axis=-1, keepdims=True)
-    grad_scores = (probs_again * (grad_probs - inner_total)).astype(bf16)
-    grad_query = (
-        jnp.einsum("shun,snhe->suhe", grad_scores, key_heads_back, preferred_element_type=f32)
-        * score_scale
-    )
-    grad_query = grad_query.astype(bf16).reshape(row_count, local_width)
-    key_part = (
-        jnp.einsum("shun,suhe->snhe", grad_scores, query_heads, preferred_element_type=f32)
-        * score_scale
-    )
-    value_part = jnp.einsum(
-        "shun,suhe->snhe", probs_low_again, grad_att_heads, preferred_element_type=f32
+    whole = ((seq_count, full_length, local_width), bf16)
+    grad_query, key_part, value_part = local_call(
+        functools.partial(attend_back_kernel, score_scale),
+        [((row_count, local_width), bf16), whole, whole],
+        [queries, key_all, value_all, probs, grad_attended],
     )
     key_grads, value_grads = scatter_blocks(
-        [x.astype(bf16).reshape(seq_count, 4, span, local_width) for x in (key_part, value_part)], False, 4
+        [x.reshape(seq_count, 4, span, local_width) for x in (key_part, value_part)], False, 4
     )
     grad_key = key_grads.astype(bf16).reshape(row_count, local_width)
     grad_value = value_grads.astype(bf16).reshape(row_count, local_width)

time: 253 us -> 229 us (0.905)
  matrix products: 31.4 us -> 14.2 us
  local copies, waits for them, and re-layouts: 32.1 us -> 16 us
  Pallas kernels: 171 us -> 182 us
    reshape x9 -> x0, local copies, waits for them, and re-layouts: 10.6 us -> none  [the longest x4 7.24 us: body(): x.astype(bf16).reshape(seq_count, 4, span, local_width)]
    pallas_call x0 -> x2, Pallas kernels: none -> 10.4 us  [local_call(): pl.pallas_call(kernel, out_shape=[jax.ShapeDtypeStruct(dims, kind) for di...]
    dot_general x5 -> x0, matrix products: 9.43 us -> none  [the longest x1 3.09 us: body(): jnp.einsum('suhe,snhe->shun', grad_att_heads, value_heads_back, preferred...]
    sub x1 -> x0, matrix products: 3.09 us -> none  [body(): expo = jnp.where(allowed, jnp.exp(masked - peak), 0.0)]
    unnamed x104 -> x89, local copies, waits for them, and re-layouts: 11.1 us -> 8.7 us
  transfers between devices with their start and end apart: 4 -> 4, of which waited for: 1 -> 0; matrix products, arithmetic and copies ran while one was open for 5% -> 6% of each run, Pallas kernels for 0% -> 0%
where the time goes in v3:
time: 229 us
  Pallas kernels  182 us (79%)
  local copies, waits for them, and re-layouts  16 us (7%)
  other arithmetic  14.9 us (7%)
  matrix products  14.2 us (6%)
    pallas_call x2, Pallas kernels, scatter_blocks(): pl.pallas_call(functools.partial(scatter_kernel, arrays, slots, z_peers),...  90 us
    pallas_call x2, Pallas kernels, gather_blocks(): pl.pallas_call(functools.partial(gather_kernel, arrays, slots, z_peers),...  81.3 us
    pallas_call x2, Pallas kernels, local_call(): pl.pallas_call(kernel, out_shape=[jax.ShapeDtypeStruct(dims, kind) for di...  10.4 us
    unnamed x89, local copies, waits for them, and re-layouts  8.7 us
  transfers between devices with their start and end apart: 4, of which 0 were waited for; matrix products, arithmetic and copies ran while one was open for 6% of the time, Pallas kernels for 0%

profile of v3, /device:TPU:0, one launch (start us, length us, event | category | flops | bytes accessed | tf_op | source)
XLA Modules:
  0.0 228.7 jit_solution(8994985008844649180)
XLA Ops:
  0.7 1.2 convert_reduce_fusion.1
  1.9 1.2 fusion.21
  3.1 0.8 slice_bitcast_fusion.6
  4.7 0.8 maximum_bitcast_fusion.refs_0_
  5.5 0.9 copy-done.8
  6.4 0.9 copy-done.9
  7.3 64.8 %shard_map.254 = (bf16[4,4,48,1536]{3,2,1,0:T(8,128)(2,1)S(1)}, bf16[4,4,48,1536]{3,2,1,0:T(8,128)(2,1)S(1)}, bf16[4,4,48,1536]{3,2,1,0:T(8,128)(2,1)S(1)}) custom-call(bf16[1,48,1536]{2,1,0:T(8,128)(2,1)S(1)} %maximum_bitcast_fusion.refs_0_, bf16[1,48,1536]{2,1,0:T(8,128)(2,1)S(1)} %bitcast.144, bf16[1,48,1536]{2,1,0:T(8,128)(2,1)S(1)} %bitcast.145), custom_call_target="tpu_custom_call" | custom-call | bytes 14155776 | tf_op jit(solution)/shard_map/pallas_call | solution.py:119
  72.1 1.4 copy-done.11
  75.0 16.5 %shard_map.255 = (bf16[2,4,128,384]{3,2,1,0:T(8,128)(2,1)S(1)}, bf16[2,4,128,384]{3,2,1,0:T(8,128)(2,1)S(1)}) custom-call(bf16[2,128,384]{2,1,0:T(8,128)(2,1)S(1)} %bitcast.136, bf16[2,128,384]{2,1,0:T(8,128)(2,1)S(1)} %bitcast.133), custom_call_target="tpu_custom_call" | custom-call | bytes 3145728 | tf_op jit(solution)/shard_map/pallas_call | solution.py:119
  91.5 5.3 %shard_map.256 = (f32[2,6,128,512]{3,2,1,0:T(8,128)S(1)}, bf16[256,384]{1,0:T(8,128)(2,1)S(1)}) custom-call(s32[2]{0:T(128)S(1)} %copy-done.10, bf16[256,384]{1,0:T(8,128)(2,1)S(1)} %get-tuple-element.66.q_ref, bf16[2,512,384]{2,1,0:T(8,128)(2,1)S(1)} %bitcast.128, bf16[2,512,384]{2,1,0:T(8,128)(2,1)S(1)} %bitcast.130), custom_call_target="tpu_custom_call" | custom-call | tf_op jit(solution)/shard_map/pallas_call | solution.py:373
  96.8 1.6 copy-done
  98.4 1.3 fusion.25
  99.7 1.9 copy.30
  101.6 1.1 convert_reduce_fusion.2
  102.8 1.8 fusion.39
  105.0 0.9 convolution_add_fusion
  106.0 2.1 convert_reduce_fusion
  108.1 0.8 fusion.41
  109.4 1.1 fusion.35
  110.6 2.4 %convolution_convert_fusion = bf16[1536,768]{0,1:T(8,128)(2,1)} fusion(bf16[256,768]{1,0:T(8,128)(2,1)S(1)} %bitcast.151, f32[256,1536]{1,0:T(8,128)S(1)} %convolution_add_fusion), kind=kOutput, calls=%fused_computation | convolution fusion | flops 608698368 | bytes 4325376 | tf_op jit(solution)/shard_map/rd,rf->df/dot_general | solution.py:435
  113.0 1.0 convolution_convert_fusion.1
  114.0 0.9 multiply_reduce_fusion
  115.0 1.3 fusion.38
  116.3 0.8 convert_reduce_fusion.3
  118.5 5.1 %shard_map.257 = (bf16[256,384]{1,0:T(8,128)(2,1)S(1)}, bf16[2,512,384]{2,1,0:T(8,128)(2,1)S(1)}, bf16[2,512,384]{2,1,0:T(8,128)(2,1)S(1)}) custom-call(bf16[256,384]{1,0:T(8,128)(2,1)S(1)} %get-tuple-element.66.q_ref, bf16[2,512,384]{2,1,0:T(8,128)(2,1)S(1)} %bitcast.129, bf16[2,512,384]{2,1,0:T(8,128)(2,1)S(1)} %bitcast.131, ...), custom_call_target="tpu_custom_call" | custom-call | tf_op jit(solution)/shard_map/pallas_call | solution.py:373
  123.6 16.1 %shard_map.258 = (f32[2,128,384]{2,1,0:T(8,128)S(1)}, f32[2,128,384]{2,1,0:T(8,128)S(1)}) custom-call(bf16[2,4,128,384]{3,2,1,0:T(8,128)(2,1)S(1)} %bitcast.134, bf16[2,4,128,384]{3,2,1,0:T(8,128)(2,1)S(1)} %bitcast.135), custom_call_target="tpu_custom_call" | custom-call | bytes 3145728 | tf_op jit(solution)/shard_map/pallas_call | solution.py:273
  139.9 1.6 fusion.7
  142.1 1.3 reshape.206
  143.8 1.7 convolution_convert_fusion.2
  146.5 1.8 fusion.36
  149.0 73.8 %shard_map.259 = (f32[1,48,1536]{2,1,0:T(8,128)S(1)}, f32[1,48,1536]{2,1,0:T(8,128)S(1)}, f32[1,48,1536]{2,1,0:T(8,128)S(1)}, f32[56,128]{1,0:T(8,128)S(1)}) custom-call(bf16[4,4,48,1536]{3,2,1,0:T(8,128)(2,1)S(1)} %pad_maximum_fusion.refs_0_, bf16[4,4,48,1536]{3,2,1,0:T(8,128)(2,1)S(1)} %bitcast.127, bf16[4,4,48,1536]{3,2,1,0:T(8,128)(2,1)S(1)} %bitcast.132, ...), custom_call_target="tpu_custom_call" | custom-call | bytes 14155776 | tf_op jit(solution)/shard_map/pallas_call | solution.py:273
  224.0 1.3 add_add_fusion.2
  (125 shorter events, 11.9 us)
Async XLA Ops:
  0.6 73.0 %copy-start.13 = (bf16[2,128,768]{2,1,0:T(8,128)(2,1)S(1)}, bf16[2,128,768]{2,1,0:T(8,128)(2,1)}, u32[]{:S(2)}) copy-start(bf16[2,128,768]{2,1,0:T(8,128)(2,1)} %param.15) | copy-start | bytes 1179652
  0.7 72.9 %copy-start.36 = (f32[768]{0:T(1024)S(1)}, f32[768]{0:T(1024)}, u32[]{:S(2)}) copy-start(f32[768]{0:T(1024)} %param.18) | copy-start | bytes 9220
  0.7 72.9 %copy-start.24 = (f32[768]{0:T(1024)S(1)}, f32[768]{0:T(1024)}, u32[]{:S(2)}) copy-start(f32[768]{0:T(1024)} %param.17) | copy-start | bytes 9220
  3.1 2.4 %copy-start.31 = (f32[2,128]{1,0:T(2,128)}, f32[2,128]{1,0:T(2,128)S(1)}, u32[]{:S(2)}) copy-start(f32[2,128]{1,0:T(2,128)S(1)} %fusion.21) | copy-start | bytes 3076
  73.6 24.8 %copy-start.6 = (bf16[4,4,48,1536]{3,2,1,0:T(8,128)(2,1)}, bf16[4,4,48,1536]{3,2,1,0:T(8,128)(2,1)S(1)}, u32[]{:S(2)}) copy-start(bf16[4,4,48,1536]{3,2,1,0:T(8,128)(2,1)S(1)} %get-tuple-element.30) | copy-start | bytes 7077892
  74.9 16.6 %copy-start.10 = (s32[2]{0:T(128)S(1)}, s32[2]{0:T(128)}, u32[]{:S(2)}) copy-start(s32[2]{0:T(128)} %lengths.1) | copy-start | bytes 28
  91.4 8.3 %copy-start.2 = (bf16[2,4,128,384]{3,2,1,0:T(8,128)(2,1)}, bf16[2,4,128,384]{3,2,1,0:T(8,128)(2,1)S(1)}, u32[]{:S(2)}) copy-start(bf16[2,4,128,384]{3,2,1,0:T(8,128)(2,1)S(1)} %get-tuple-element.32) | copy-start | bytes 2359300
  99.7 3.0 %collective-permute-start = (f32[256,768]{1,0:T(8,128)}, f32[256,768]{1,0:T(8,128)}, u32[]{:S(2)}, u32[]{:S(2)}) collective-permute-start(f32[256,768]{1,0:T(8,128)} %fusion.25), channel_id=1, source_target_pairs={{0,1},{1,0},{2,3},{3,2},{4,5},{5,4},{6,7},{7,6},{8,9},{9,8},{10,11... | collective-permute-start | bytes 2359304 | tf_op jit(solution)/shard_map/ppermute | solution.py:298
  102.7 2.3 copy-start.12
  102.7 2.3 copy-start.25
  102.7 2.3 copy-start.37
  102.7 2.2 copy-start.39
  108.9 5.1 %collective-permute-start.2 = (f32[256,768]{1,0:T(8,128)S(1)}, f32[256,768]{1,0:T(8,128)S(1)}, u32[]{:S(2)}, u32[]{:S(2)}) collective-permute-start(f32[256,768]{1,0:T(8,128)S(1)} %fusion.41), channel_id=1, source_target_pairs={{0,1},{1,0},{2,3},{3,2},{4,5},{5,4},{6,7},{7,6},{8,9},{9,8},{10,11... | collective-permute-start | bytes 2359304 | tf_op jit(solution)/shard_map/ppermute | solution.py:298
  110.5 4.5 %collective-permute-start.1 = (f32[256,768]{1,0:T(8,128)S(1)}, f32[256,768]{1,0:T(8,128)S(1)}, u32[]{:S(2)}, u32[]{:S(2)}) collective-permute-start(f32[256,768]{1,0:T(8,128)S(1)} %fusion.35), channel_id=1, source_target_pairs={{0,1},{1,0},{2,3},{3,2},{4,5},{5,4},{6,7},{7,6},{8,9},{9,8},{10,11... | collective-permute-start | bytes 2359304 | tf_op jit(solution)/shard_map/ppermute | solution.py:298
  115.0 2.1 copy-start.7
  115.0 3.0 %copy-start.1 = (f32[2,6,128,512]{3,2,1,0:T(8,128)S(1)}, f32[2,6,128,512]{3,2,1,0:T(8,128)}, u32[]{:S(2)}) copy-start(f32[2,6,128,512]{3,2,1,0:T(8,128)} %copy-done) | copy-start | bytes 9437188
  116.3 2.2 copy-start.3
  123.6 17.9 %copy-start.5 = (bf16[256,384]{1,0:T(8,128)(2,1)}, bf16[256,384]{1,0:T(8,128)(2,1)S(1)}, u32[]{:S(2)}) copy-start(bf16[256,384]{1,0:T(8,128)(2,1)S(1)} %get-tuple-element.37) | copy-start | bytes 589828
  139.9 3.5 %copy-start.21 = (bf16[256,768]{1,0:T(8,128)(2,1)S(1)}, bf16[256,768]{1,0:T(8,128)(2,1)}, u32[]{:S(2)}) copy-start(bf16[256,768]{1,0:T(8,128)(2,1)} %copy-done.20) | copy-start | bytes 1179652
  139.9 3.9 %copy-start.22 = (bf16[768,256]{1,0:T(8,128)(2,1)S(1)}, bf16[768,256]{1,0:T(8,128)(2,1)}, u32[]{:S(2)}) copy-start(bf16[768,256]{1,0:T(8,128)(2,1)} %copy.30) | copy-start | bytes 1179652
  141.5 4.4 %collective-permute-start.3 = (f32[256,768]{1,0:T(8,128)}, f32[256,768]{1,0:T(8,128)}, u32[]{:S(2)}, u32[]{:S(2)}) collective-permute-start(f32[256,768]{1,0:T(8,128)} %fusion.7), channel_id=1, source_target_pairs={{0,1},{1,0},{2,3},{3,2},{4,5},{5,4},{6,7},{7,6},{8,9},{9,8},{10,11... | collective-permute-start | bytes 2359304 | tf_op jit(solution)/shard_map/ppermute | solution.py:298
  145.8 2.5 %copy-start.32 = (f32[2,128]{1,0:T(2,128)S(1)}, f32[2,128]{1,0:T(2,128)}, u32[]{:S(2)}) copy-start(f32[2,128]{1,0:T(2,128)} %copy-done.31) | copy-start | bytes 3076
  145.8 2.9 %copy-start.26 = (f32[6912]{0:T(1024)S(1)}, f32[6912]{0:T(1024)}, u32[]{:S(2)}) copy-start(f32[6912]{0:T(1024)} %custom-call) | copy-start | bytes 82948
  145.8 3.0 %copy-start.30 = (f32[768]{0:T(1024)S(1)}, f32[768]{0:T(1024)}, u32[]{:S(2)}) copy-start(f32[768]{0:T(1024)} %reshape.206) | copy-start | bytes 9220
  145.8 3.0 %copy-start.29 = (f32[768]{0:T(1024)S(1)}, f32[768]{0:T(1024)}, u32[]{:S(2)}) copy-start(f32[768]{0:T(1024)} %get-tuple-element.55) | copy-start | bytes 9220
  145.8 3.0 %copy-start.28 = (f32[768]{0:T(1024)S(1)}, f32[768]{0:T(1024)}, u32[]{:S(2)}) copy-start(f32[768]{0:T(1024)} %get-tuple-element.46) | copy-start | bytes 9220
  145.8 3.0 %copy-start.27 = (f32[768]{0:T(1024)S(1)}, f32[768]{0:T(1024)}, u32[]{:S(2)}) copy-start(f32[768]{0:T(1024)} %get-tuple-element.50) | copy-start | bytes 9220
  145.9 3.0 %copy-start.35 = (f32[1536]{0:T(1024)S(1)}, f32[1536]{0:T(1024)}, u32[]{:S(2)}) copy-start(f32[1536]{0:T(1024)} %get-tuple-element.84) | copy-start | bytes 18436
  145.9 3.0 %copy-start.4 = (bf16[1536,768]{0,1:T(8,128)(2,1)S(1)}, bf16[1536,768]{0,1:T(8,128)(2,1)}, u32[]{:S(2)}) copy-start(bf16[1536,768]{0,1:T(8,128)(2,1)} %convolution_convert_fusion) | copy-start | bytes 7077892
  148.9 75.1 %copy-start.16 = (f32[256,768]{1,0:T(8,128)S(1)}, f32[256,768]{1,0:T(8,128)}, u32[]{:S(2)}) copy-start(f32[256,768]{1,0:T(8,128)} %copy-done.15) | copy-start | bytes 2359300
  148.9 75.1 %copy-start.18 = (bf16[2,128,768]{2,1,0:T(8,128)(2,1)S(1)}, bf16[2,128,768]{2,1,0:T(8,128)(2,1)}, u32[]{:S(2)}) copy-start(bf16[2,128,768]{2,1,0:T(8,128)(2,1)} %param.29) | copy-start | bytes 1179652
  148.9 75.1 %copy-start.34 = (f32[256]{0:T(256)S(1)}, f32[256]{0:T(256)}, u32[]{:S(2)}) copy-start(f32[256]{0:T(256)} %copy-done.33) | copy-start | bytes 3076
  (12 other events, 13.8 us)
